TPU v7x, 32 devices: a whole 2x2x4 slice. The times are simulated.
32 devices in a mesh: dp: 4 (over y, x), expert: 8 (over z, core).
Axes of the slice: x: 2, y: 2, z: 4, core: 2. Of those that a mesh axis runs over, the one named last changes fastest.
Arguments:
- tokens: bfloat16 [73728, 512], P(('dp', 'expert')), may hold values from -6 to 6
- gain_one: float32 [512], replicated, may hold values from 0.1 to 1.9
- w_qkv: bfloat16 [512, 1536], replicated, may hold values from -0.25 to 0.25
- w_attn_out: bfloat16 [512, 512], replicated, may hold values from -1 to 1
- gain_two: float32 [512], replicated, may hold values from 0.1 to 1.9
- w_router: bfloat16 [512, 8], replicated, may hold values from -0.1875 to 0.1875
- w_first: bfloat16 [8, 512, 2048], P('expert'), may hold values from -0.25 to 0.25
- w_second: bfloat16 [8, 2048, 512], P('expert'), may hold values from -1 to 1
- expert_ids: int32 [73728, 2], P(('dp', 'expert')), may hold values from 0 to 7, all different within a row
- priority_ranks: int32 [32, 2304], P(('dp', 'expert')), may hold values from 0 to 2303, each once within a row
- cotangent: float32 [73728, 512], P(('dp', 'expert')), may hold values from -6 to 6
Outputs:
- block_out: bfloat16 [73728, 512], P(('dp', 'expert'))
- grad_tokens: float32 [73728, 512], P(('dp', 'expert'))
- grad_gain_one: float32 [512], replicated
- grad_w_qkv: float32 [512, 1536], replicated
- grad_w_attn_out: float32 [512, 512], replicated
- grad_gain_two: float32 [512], replicated
- grad_w_router: float32 [512, 8], replicated
- grad_w_first: float32 [8, 512, 2048], P('expert')
- grad_w_second: float32 [8, 2048, 512], P('expert')
Inputs may be any that keep to these rules, and one draw needn't show every extreme that they name: `expert_ids`: each row names two different experts, and every expert is named somewhere. `priority_ranks`: each row is a permutation of 0 to 2303.
All inputs are finite; a program needn't handle non-finite values.
Results may differ from a plain program's by a relative error of at most 0.015.
Values may be sent and summed in bfloat16 or wider, within the bound.
No kernel may reach another device: no remote copies, remote signals or barrier semaphores. Data moves between devices by JAX's collectives and lax.ppermute only.
A program may use at most 256 MiB of HBM per device.

v0:
```python
from functools import partial

import jax
import jax.numpy as jnp
from jax import lax
from jax.experimental import pallas as pl
from jax.experimental.pallas import tpu as pltpu
from jax.sharding import Mesh
from jax.sharding import PartitionSpec as P

D = 512
HEADS = 8
HEAD_DIM = 64
PATCHES = 144
QUAD = 256
EPSILON = 1e-06
EXTRA = 16
SMALL = 8
LANES = 128
F32 = jnp.float32
BF16 = jnp.bfloat16
VMEM_LIMIT = 60 * 1024 * 1024


def nn(a, b):
    return lax.dot_general(a, b, (((1,), (0,)), ((), ())), preferred_element_type=F32)


def nt(a, b):
    return lax.dot_general(a, b, (((1,), (1,)), ((), ())), preferred_element_type=F32)


def tn(a, b):
    return lax.dot_general(a, b, (((0,), (0,)), ((), ())), preferred_element_type=F32)


def standardise(values):
    average = jnp.mean(values, axis=-1, keepdims=True)
    centred = values - average
    variance = jnp.mean(centred * centred, axis=-1, keepdims=True)
    inverse = lax.rsqrt(variance + EPSILON)
    return centred * inverse, inverse


def standardise_back(hat, inverse, gain, grad):
    scaled = grad * gain
    mean_one = jnp.mean(scaled, axis=-1, keepdims=True)
    mean_two = jnp.mean(scaled * hat, axis=-1, keepdims=True)
    return inverse * (scaled - mean_one - hat * mean_two)


def halves(values):
    high = values.astype(BF16)
    low = (values - high.astype(F32)).astype(BF16)
    return high, low


def params(**more):
    return pltpu.CompilerParams(vmem_limit_bytes=VMEM_LIMIT, **more)


def whole(shape):
    zeros = (0,) * len(shape)
    return pl.BlockSpec(shape, lambda *_: zeros)


def route_kernel(experts, capacity, stride, ids_ref, ranks_ref, out_ref, cols_ref):
    toks = ids_ref.shape[1]
    catalog = lax.broadcasted_iota(jnp.int32, (experts, toks), 0)
    first_hot = (ids_ref[0:1, :] == catalog).astype(F32)
    second_hot = (ids_ref[1:2, :] == catalog).astype(F32)
    both = jnp.concatenate([first_hot, second_hot], axis=0).astype(BF16)
    first_total = jnp.sum(first_hot, axis=1, keepdims=True)
    ranks = ranks_ref[...].astype(F32)
    rank_rows = jnp.broadcast_to(ranks, (8, toks))
    rank_cols = jnp.transpose(rank_rows)[:, 0:1]
    tile = 256
    for start in range(0, toks, tile):
        part = slice(start, start + tile)
        earlier = (rank_cols < ranks[:, part]).astype(F32).astype(BF16)
        counted = nn(both, earlier)
        slot_first = jnp.sum(counted[:experts] * first_hot[:, part], axis=0, keepdims=True)
        slot_second = jnp.sum(
            (counted[experts:] + first_total) * second_hot[:, part], axis=0, keepdims=True
        )
        for row, slot in ((0, slot_first), (1, slot_second)):
            slot = slot.astype(jnp.int32)
            flat = ids_ref[row : row + 1, part] * stride + slot
            out_ref[row : row + 1, part] = jnp.where(slot < capacity, flat, -1)
    out_ref[2:, :] = jnp.full((6, toks), -1, jnp.int32)
    cols_ref[...] = jnp.transpose(out_ref[...].astype(F32)).astype(jnp.int32)


def route(ids, ranks, experts, capacity, stride):
    toks = ranks.shape[1]
    return pl.pallas_call(
        partial(route_kernel, experts, capacity, stride),
        out_shape=(
            jax.ShapeDtypeStruct((8, toks), jnp.int32),
            jax.ShapeDtypeStruct((toks, 8), jnp.int32),
        ),
        in_specs=[whole((2, toks)), whole((1, toks))],
        out_specs=(whole((8, toks)), whole((toks, 8))),
        grid=(1,),
        compiler_params=params(),
        name="route",
        cost_estimate=pl.CostEstimate(
            flops=2 * toks * toks * 128, bytes_accessed=toks * 48, transcendentals=0
        ),
    )(ids, ranks)


def selector_rows(base, rows, flat_ref):
    toks = flat_ref.shape[1]
    slot = lax.broadcasted_iota(jnp.int32, (rows, toks), 0) + base
    hit = (slot == flat_ref[0:1, :]) | (slot == flat_ref[1:2, :])
    return jnp.where(hit, 1.0, 0.0).astype(BF16)


def dispatch_grad_kernel(stride, mine_ref, flat_ref, grad_ref, out_ref, low_ref):
    step = pl.program_id(0)

    @pl.when(step == 0)
    def _():
        low_ref[...] = grad_ref[...].astype(BF16)

    chosen = selector_rows((step ^ mine_ref[0]) * stride, out_ref.shape[1], flat_ref)
    out_ref[0] = nn(chosen, low_ref[...]).astype(BF16)


def dispatch_grad(mine, flat, grad, experts, rows, stride):
    toks = grad.shape[0]
    return pl.pallas_call(
        partial(dispatch_grad_kernel, stride),
        out_shape=jax.ShapeDtypeStruct((experts, rows, D), BF16),
        in_specs=[pl.BlockSpec(memory_space=pltpu.SMEM), whole((8, toks)), whole((toks, D))],
        out_specs=pl.BlockSpec((1, rows, D), lambda e: (e, 0, 0)),
        grid=(experts,),
        scratch_shapes=[pltpu.VMEM((toks, D), BF16)],
        compiler_params=params(),
        name="dispatch_grad",
        cost_estimate=pl.CostEstimate(
            flops=4 * toks * experts * rows * D, bytes_accessed=toks * D * 6, transcendentals=0
        ),
    )(mine, flat, grad)


def dispatch_kernel(stride, steps, flat_ref, low_ref, *out_refs):
    for k, out_ref in zip(steps, out_refs):
        chosen = selector_rows(k * stride, out_ref.shape[0], flat_ref)
        out_ref[...] = nn(chosen, low_ref[...]).astype(BF16)


def dispatch(flat, low, steps, rows, stride):
    toks = low.shape[0]
    return pl.pallas_call(
        partial(dispatch_kernel, stride, steps),
        out_shape=(jax.ShapeDtypeStruct((rows, D), BF16),) * len(steps),
        in_specs=[whole((8, toks)), whole((toks, D))],
        out_specs=(whole((rows, D)),) * len(steps),
        grid=(1,),
        compiler_params=params(),
        name="dispatch",
        cost_estimate=pl.CostEstimate(
            flops=4 * toks * len(steps) * rows * D, bytes_accessed=toks * D * 4, transcendentals=0
        ),
    )(flat, low)


def rows_of(wide, rows):
    flipped = jnp.transpose(wide)[:EXTRA]
    return jnp.concatenate([flipped, jnp.zeros((EXTRA, D - rows), F32)], axis=1).astype(BF16)


def columns_of(extra, rows):
    flipped = jnp.transpose(extra.astype(F32))
    return flipped[:rows, 0:1] + flipped[:rows, 1:2]


def router_softmax(low, router_w, experts):
    logits = nn(low, router_w)
    lane = lax.broadcasted_iota(jnp.int32, logits.shape, 1)
    logits = jnp.where(lane < experts, logits, -1e30)
    raised = jnp.exp(logits - jnp.max(logits, axis=1, keepdims=True))
    return raised / jnp.sum(raised, axis=1, keepdims=True)


def head_stack(values):
    lane = lax.broadcasted_iota(jnp.int32, values.shape, 1) // HEAD_DIM
    zero = jnp.zeros_like(values)
    return jnp.concatenate([jnp.where(lane == h, values, zero) for h in range(4)], axis=0)


def forward_kernel(
    experts,
    x_ref,
    gain_one_ref,
    qkv_ref,
    out_w_ref,
    gain_two_ref,
    router_w_ref,
    packed_ref,
    log_ref,
    mixed_ref,
    resid_ref,
    low_two_ref,
    router_ref,
):
    images = log_ref.shape[0]
    x = x_ref[...].astype(F32)
    hat, _ = standardise(x)
    low_one = (hat * gain_one_ref[...]).astype(BF16)
    packed_ref[...] = nn(low_one, qkv_ref[...]).astype(BF16)
    for image in range(images):
        rows = slice(image * PATCHES, (image + 1) * PATCHES)
        for quad in range(2):
            cols = slice(quad * QUAD, (quad + 1) * QUAD)
            queries = packed_ref[rows, quad * QUAD : quad * QUAD + QUAD] * HEAD_DIM ** (-0.5)
            keys = packed_ref[rows, D + quad * QUAD : D + quad * QUAD + QUAD]
            values = packed_ref[rows, 2 * D + quad * QUAD : 2 * D + quad * QUAD + QUAD]
            values_t = jnp.transpose(values)
            scores = nt(head_stack(keys), queries.astype(BF16))
            parts = []
            for h in range(4):
                own = scores[h * PATCHES : (h + 1) * PATCHES]
                top = jnp.max(own, axis=0, keepdims=True)
                weights = jnp.exp(own - top)
                total = jnp.sum(weights, axis=0, keepdims=True)
                log_ref[image, quad * 4 + h : quad * 4 + h + 1, :] = top + jnp.log(total)
                part = nn(values_t[h * HEAD_DIM : (h + 1) * HEAD_DIM], weights.astype(BF16))
                parts.append(part / total)
            mixed_t = jnp.concatenate(parts, axis=0)
            mixed_ref[rows, cols] = jnp.transpose(mixed_t).astype(BF16)
    resid = x + nn(mixed_ref[...], out_w_ref[...])
    resid_ref[...] = resid
    hat_two, _ = standardise(resid)
    low_two = (hat_two * gain_two_ref[...]).astype(BF16)
    low_two_ref[...] = low_two
    router_ref[...] = router_softmax(low_two, router_w_ref[...], experts)


def attention_forward(x, gain_one, qkv, out_w, gain_two, router_w, experts, block):
    toks = x.shape[0]
    rows = block * PATCHES
    images = toks // PATCHES

    def tile(width):
        return pl.BlockSpec((rows, width), lambda i: (i, 0))

    return pl.pallas_call(
        partial(forward_kernel, experts),
        out_shape=(
            jax.ShapeDtypeStruct((toks, 3 * D), BF16),
            jax.ShapeDtypeStruct((images, HEADS, PATCHES), F32),
            jax.ShapeDtypeStruct((toks, D), BF16),
            jax.ShapeDtypeStruct((toks, D), F32),
            jax.ShapeDtypeStruct((toks, D), BF16),
            jax.ShapeDtypeStruct((toks, LANES), F32),
        ),
        in_specs=[
            tile(D),
            whole((1, D)),
            whole((D, 3 * D)),
            whole((D, D)),
            whole((1, D)),
            whole((D, LANES)),
        ],
        out_specs=(
            tile(3 * D),
            pl.BlockSpec((block, HEADS, PATCHES), lambda i: (i, 0, 0)),
            tile(D),
            tile(D),
            tile(D),
            tile(LANES),
        ),
        grid=(images // block,),
        compiler_params=params(),
        name="attention_forward",
        cost_estimate=pl.CostEstimate(
            flops=31_000_000_000, bytes_accessed=toks * D * 20, transcendentals=0
        ),
    )(x, gain_one, qkv, out_w, gain_two, router_w)


GELU_C = 0.7978845608028654
GELU_A = 0.044715


def gelu_pair(v):
    square = v * v
    inner = v * (GELU_C + (GELU_C * GELU_A) * square)
    curve = jnp.tanh(inner)
    half = 0.5 + 0.5 * curve
    slope = half + 0.5 * v * (1.0 - curve * curve) * (GELU_C + (3.0 * GELU_C * GELU_A) * square)
    return v * half, slope


def expert_kernel(experts, count, choices, sources_ref, lane_ref, pick_ref, *refs):
    received_refs = refs[:count]
    grad_ref, router_w_ref = refs[count : count + 2]
    first_choices = refs[count + 2 : count + 2 + choices]
    second_choices = refs[count + 2 + choices : count + 2 + 2 * choices]
    first_ref, second_ref, sem = refs[-3:]
    outs = refs[len(refs) - 3 - count - 5 : -3]
    back_refs = outs[:count]
    out_ref, hidden_ref, d_pre_ref, d_out_ref, low_ref = outs[count:]
    step = pl.program_id(0)

    @pl.when(step == 0)
    def _():
        for at, from_refs, to_ref in ((0, first_choices, first_ref), (1, second_choices, second_ref)):
            for n, from_ref in enumerate(from_refs):

                @pl.when(pick_ref[at] == n)
                def _():
                    pltpu.make_async_copy(from_ref, to_ref, sem.at[at]).start()

        pltpu.make_async_copy(first_choices[0], first_ref, sem.at[0]).wait()
        pltpu.make_async_copy(second_choices[0], second_ref, sem.at[1]).wait()

    rows = low_ref.shape[0]
    hidden_cols = first_ref.shape[2]
    for r in range(count):

        @pl.when(step == r)
        def _():
            low_ref[...] = received_refs[r][...]

    lane = lax.broadcasted_iota(jnp.int32, (rows, LANES), 1)
    router = router_softmax(low_ref[...], router_w_ref[...], experts)
    gate = jnp.sum(jnp.where(lane == lane_ref[0], router, 0.0), axis=1, keepdims=True)
    d_out_ref[...] = (gate * grad_ref[0].astype(F32)).astype(BF16)
    chunk = 256
    parts = [slice(start, start + chunk) for start in range(0, hidden_cols, chunk)]
    low = low_ref[...]
    d_out = d_out_ref[...]

    def ahead(part):
        return nn(low, first_ref[0, :, part]), nt(d_out, second_ref[0, part, :])

    out = None
    back = None
    later = ahead(parts[0])
    for n, part in enumerate(parts):
        pre, d_hidden = later
        if n + 1 < len(parts):
            later = ahead(parts[n + 1])
        act, slope = gelu_pair(pre)
        act = act.astype(BF16)
        d_pre = (d_hidden * slope).astype(BF16)
        hidden_ref[:, part] = act
        d_pre_ref[:, part] = d_pre
        piece = nn(act, second_ref[0, part, :])
        out = piece if out is None else out + piece
        piece = nt(d_pre, first_ref[0, :, part])
        back = piece if back is None else back + piece
    given = out.astype(BF16)
    out_ref[0] = given
    d_gate = jnp.sum(given.astype(F32) * grad_ref[0].astype(F32), axis=1, keepdims=True)
    high = d_gate.astype(BF16).astype(F32)
    wide = jnp.where(lane == 0, high, jnp.where(lane == 1, d_gate - high, 0.0))
    extra = rows_of(wide, rows)
    back = back.astype(BF16)
    for r in range(count):

        @pl.when(step == r)
        def _():
            back_refs[r][:rows] = back
            back_refs[r][rows:] = extra


def expert_apply(at, sources, lane, received, grad, weights, router_w, experts, stride, kept):
    pick, first, second = weights
    groups, rows, _ = grad.shape
    wide = first[0].shape[2]
    total = groups * rows
    count = len(received)

    def flat(width):
        return pl.BlockSpec((rows, width), lambda j, *_: (at + j, 0))

    kept_shapes = (
        jax.ShapeDtypeStruct((groups, rows, D), BF16),
        jax.ShapeDtypeStruct((total, wide), BF16),
        jax.ShapeDtypeStruct((total, wide), BF16),
        jax.ShapeDtypeStruct((total, D), BF16),
        jax.ShapeDtypeStruct((total, D), BF16),
    )
    source = pl.BlockSpec((1, rows, D), lambda j, sources, *_: (sources[j], 0, 0))
    anywhere = pl.BlockSpec(memory_space=pl.ANY)
    given = count + 5 + 2 * len(first)
    results = pl.pallas_call(
        partial(expert_kernel, experts, count, len(first)),
        out_shape=(jax.ShapeDtypeStruct((stride, D), BF16),) * count + kept_shapes,
        grid_spec=pltpu.PrefetchScalarGridSpec(
            num_scalar_prefetch=3,
            in_specs=[whole((rows, D))] * count
            + [source, whole((D, LANES))]
            + [anywhere] * (2 * len(first) + len(kept)),
            out_specs=(whole((stride, D)),) * count
            + (source, flat(wide), flat(wide), flat(D), flat(D)),
            grid=(count,),
            scratch_shapes=[
                pltpu.VMEM((1, D, wide), BF16),
                pltpu.VMEM((1, wide, D), BF16),
                pltpu.SemaphoreType.DMA((2,)),
            ],
        ),
        input_output_aliases={given + n: count + n for n in range(len(kept))},
        compiler_params=params(),
        name="expert_apply",
        cost_estimate=pl.CostEstimate(
            flops=15 * count * rows * D * wide,
            bytes_accessed=count * rows * wide * 4,
            transcendentals=0,
        ),
    )(sources, lane, pick, *received, grad, router_w, *first, *second, *kept)
    return results[:count], results[count:]


def expert_grads_kernel(core_ref, low_ref, d_out_ref, hidden_ref, d_pre_ref, keep_ref, give_ref):
    first = tn(low_ref[...], d_pre_ref[...]).astype(BF16)
    second = tn(hidden_ref[...], d_out_ref[...]).astype(BF16)
    even = core_ref[0] == 0

    @pl.when(even)
    def _():
        keep_ref[0] = first
        give_ref[0] = second

    @pl.when(jnp.logical_not(even))
    def _():
        keep_ref[0] = second
        give_ref[0] = first


def expert_grads(core, low, d_out, hidden, d_pre):
    total, wide = hidden.shape
    block = pl.BlockSpec((1, D, D), lambda i: (i, 0, 0))
    return pl.pallas_call(
        expert_grads_kernel,
        out_shape=(jax.ShapeDtypeStruct((wide // D, D, D), BF16),) * 2,
        in_specs=[
            pl.BlockSpec(memory_space=pltpu.SMEM),
            whole((total, D)),
            whole((total, D)),
            pl.BlockSpec((total, D), lambda i: (0, i)),
            pl.BlockSpec((total, D), lambda i: (0, i)),
        ],
        out_specs=(block, block),
        grid=(wide // D,),
        compiler_params=params(),
        name="expert_grads",
        cost_estimate=pl.CostEstimate(
            flops=8 * total * D * wide, bytes_accessed=total * wide * 4, transcendentals=0
        ),
    )(core, low, d_out, hidden, d_pre)


def pair_kernel(picks_ref, keep_ref, got_ref, *out_refs):
    step = pl.program_id(0)
    total = (keep_ref[0].astype(F32) + got_ref[0].astype(F32)).astype(BF16)
    for r, out_ref in enumerate(out_refs):

        @pl.when(step == r)
        def _():
            out_ref[...] = total


def pair_quarters(picks, keep, got):
    quarter = pl.BlockSpec((1, D, D), lambda i, picks: (picks[i], 0, 0))
    return pl.pallas_call(
        pair_kernel,
        out_shape=(jax.ShapeDtypeStruct((D, D), BF16),) * 4,
        grid_spec=pltpu.PrefetchScalarGridSpec(
            num_scalar_prefetch=1,
            in_specs=[quarter, quarter],
            out_specs=(pl.BlockSpec((D, D), lambda i, picks: (0, 0)),) * 4,
            grid=(4,),
        ),
        compiler_params=params(),
        name="pair_quarters",
        cost_estimate=pl.CostEstimate(flops=D * D, bytes_accessed=D * D * 24, transcendentals=0),
    )(picks, keep, got)


def join_kernel(turn_ref, a_ref, b_ref, c_ref, d_ref, own_a_ref, own_c_ref, out_ref):
    def total(one_ref, two_ref, own_ref, flag):
        own = jnp.where(flag != 0, own_ref[...].astype(F32), 0.0)
        return (one_ref[...].astype(F32) + two_ref[...].astype(F32) + own).astype(BF16)

    left = total(a_ref, b_ref, own_a_ref, turn_ref[1])
    right = total(c_ref, d_ref, own_c_ref, turn_ref[2])
    straight = turn_ref[0] == 0

    @pl.when(straight)
    def _():
        out_ref[0] = left
        out_ref[1] = right

    @pl.when(jnp.logical_not(straight))
    def _():
        out_ref[0] = right
        out_ref[1] = left


def join_quarters(turn, pieces):
    return pl.pallas_call(
        join_kernel,
        out_shape=jax.ShapeDtypeStruct((2, D, D), BF16),
        in_specs=[pl.BlockSpec(memory_space=pltpu.SMEM)] + [whole((D, D))] * 6,
        out_specs=whole((2, D, D)),
        grid=(1,),
        compiler_params=params(),
        name="join_quarters",
        cost_estimate=pl.CostEstimate(flops=D * D, bytes_accessed=D * D * 12, transcendentals=0),
    )(turn, *pieces)


def unfold_kernel(corner_ref, *refs):
    first_ref, second_ref = refs[-2:]
    step = pl.program_id(0)
    for r in range(4):

        @pl.when(step == r)
        def _():
            first_ref[0] = refs[r][0].astype(F32)
            second_ref[0] = refs[r][1].astype(F32)


def unfold(corner, pieces):
    return pl.pallas_call(
        unfold_kernel,
        out_shape=(
            jax.ShapeDtypeStruct((1, D, 4 * D), F32),
            jax.ShapeDtypeStruct((1, 4 * D, D), F32),
        ),
        grid_spec=pltpu.PrefetchScalarGridSpec(
            num_scalar_prefetch=1,
            in_specs=[pl.BlockSpec((2, D, D), lambda i, corner: (0, 0, 0))] * 4,
            out_specs=(
                pl.BlockSpec((1, D, D), lambda i, corner: (0, 0, i ^ corner[0])),
                pl.BlockSpec((1, D, D), lambda i, corner: (0, i ^ corner[0], 0)),
            ),
            grid=(4,),
        ),
        compiler_params=params(),
        name="unfold",
        cost_estimate=pl.CostEstimate(
            flops=400_000 * D * D, bytes_accessed=D * D * 48, transcendentals=0
        ),
    )(corner, *pieces)


def selector_cols(first, second, slots):
    slot = lax.broadcasted_iota(jnp.int32, (first.shape[0], slots), 1)
    hit = (slot == first) | (slot == second)
    return jnp.where(hit, 1.0, 0.0).astype(BF16)


def backward_kernel(experts, capacity_rows, *refs):
    backward_body(experts, capacity_rows, refs[:experts], *refs[experts:])


def backward_body(
    experts,
    capacity_rows,
    back_refs,
    flat_ref,
    cot_ref,
    resid_ref,
    router_ref,
    low_two_ref,
    mixed_ref,
    packed_ref,
    log_ref,
    x_ref,
    gain_one_ref,
    gain_two_ref,
    router_w_ref,
    out_w_ref,
    order_ref,
    core_ref,
    d_resid_ref,
    d_packed_ref,
    keep_ref,
    give_ref,
    returned_ref,
    gate_ref,
    qkv_grad_ref,
    out_grad_ref,
    router_grad_ref,
    gain_two_grad_ref,
):
    step = pl.program_id(0)
    stride = capacity_rows + EXTRA
    slots = experts * stride

    @pl.when(step == 0)
    def _():
        lane = lax.broadcasted_iota(jnp.int32, (capacity_rows, LANES), 1)
        for e in range(experts):
            base = e * stride
            returned_ref[base : base + stride] = back_refs[e][...]
            column = columns_of(back_refs[e][capacity_rows:, :], capacity_rows)
            high = column.astype(BF16).astype(F32)
            wide = jnp.where(
                lane == e, high, jnp.where(lane == experts + e, column - high, 0.0)
            )
            gate_ref[base : base + capacity_rows] = wide.astype(BF16)
            gate_ref[base + capacity_rows : base + stride] = jnp.zeros((EXTRA, LANES), BF16)
        qkv_grad_ref[...] = jnp.zeros_like(qkv_grad_ref)
        out_grad_ref[...] = jnp.zeros_like(out_grad_ref)
        router_grad_ref[...] = jnp.zeros_like(router_grad_ref)
        gain_two_grad_ref[...] = jnp.zeros_like(gain_two_grad_ref)

    first, second = flat_ref[:, 0:1], flat_ref[:, 1:2]
    chosen = selector_cols(first, second, slots)
    d_two = nn(chosen, returned_ref[...])
    d_router = nn(chosen, gate_ref[...])
    d_router = d_router + pltpu.roll(d_router, LANES - experts, 1)
    router = router_ref[...]
    d_logits = router * (d_router - jnp.sum(router * d_router, axis=1, keepdims=True))
    high, low = halves(d_logits)
    d_two = d_two + nt(high, router_w_ref[...]) + nt(low, router_w_ref[...])
    low_two = low_two_ref[...]
    router_grad_ref[...] += tn(high, low_two) + tn(low, low_two)
    hat_two, inverse_two = standardise(resid_ref[...])
    gain_two_grad_ref[...] += jnp.sum(d_two * hat_two, axis=0, keepdims=True)
    d_resid = cot_ref[...] + standardise_back(hat_two, inverse_two, gain_two_ref[...], d_two)
    d_resid_ref[...] = d_resid
    d_attn = d_resid.astype(BF16)
    out_grad_ref[...] += tn(mixed_ref[...], d_attn)
    d_mixed = nt(d_attn, out_w_ref[...]).astype(BF16)
    scale = HEAD_DIM ** (-0.5)
    images = log_ref.shape[0]
    for image in range(images):
        rows = slice(image * PATCHES, (image + 1) * PATCHES)
        for quad in range(2):
            at = quad * QUAD
            queries = packed_ref[rows, at : at + QUAD] * scale
            queries = queries.astype(BF16)
            keys = packed_ref[rows, D + at : D + at + QUAD]
            values = packed_ref[rows, 2 * D + at : 2 * D + at + QUAD]
            grads = d_mixed[rows, at : at + QUAD]
            scores = nt(head_stack(keys), queries)
            d_probs = nt(head_stack(values), grads)
            keys_t = jnp.transpose(keys)
            lane = lax.broadcasted_iota(jnp.int32, (PATCHES, QUAD), 1) // HEAD_DIM
            d_values = jnp.zeros((PATCHES, QUAD), F32)
            d_keys = jnp.zeros((PATCHES, QUAD), F32)
            parts = []
            for h in range(4):
                own = slice(h * PATCHES, (h + 1) * PATCHES)
                log_row = log_ref[image, quad * 4 + h : quad * 4 + h + 1, :]
                probs = jnp.exp(scores[own] - log_row)
                d_own = d_probs[own]
                inner = jnp.sum(probs * d_own, axis=0, keepdims=True)
                d_scores = (probs * (d_own - inner)).astype(BF16)
                d_values = jnp.where(lane == h, nn(probs.astype(BF16), grads), d_values)
                d_keys = jnp.where(lane == h, nn(d_scores, queries), d_keys)
                parts.append(nn(keys_t[h * HEAD_DIM : (h + 1) * HEAD_DIM], d_scores))
            d_queries = jnp.transpose(jnp.concatenate(parts, axis=0)) * scale
            d_packed_ref[rows, at : at + QUAD] = d_queries.astype(BF16)
            d_packed_ref[rows, D + at : D + at + QUAD] = d_keys.astype(BF16)
            d_packed_ref[rows, 2 * D + at : 2 * D + at + QUAD] = d_values.astype(BF16)
    hat_one, _ = standardise(x_ref[...].astype(F32))
    low_one = (hat_one * gain_one_ref[...]).astype(BF16)
    qkv_grad_ref[...] += tn(low_one, d_packed_ref[...])

    @pl.when(step == pl.num_programs(0) - 1)
    def _():
        count, height, _ = keep_ref.shape
        piece = height - SMALL
        high, low = halves(router_grad_ref[...])
        router_grad = nn(order_ref[...], high) + nn(order_ref[...], low)
        small = jnp.concatenate(
            [router_grad[:experts], jnp.broadcast_to(gain_two_grad_ref[...], (SMALL, D))],
            axis=0,
        ).astype(BF16)

        def spread(low_ref, high_ref):
            for j in range(2 * count):
                target = low_ref if j < count else high_ref
                block, at = divmod(j * piece, D)
                if block < 3:
                    rows = qkv_grad_ref[at : at + piece, block * D : (block + 1) * D]
                else:
                    rows = out_grad_ref[at : at + piece, :]
                target[j % count, :piece] = rows.astype(BF16)
                if j * SMALL < experts + SMALL:
                    target[j % count, piece:] = small[j * SMALL : (j + 1) * SMALL]
                else:
                    target[j % count, piece:] = jnp.zeros((SMALL, D), BF16)

        @pl.when(core_ref[0] == 0)
        def _():
            spread(keep_ref, give_ref)

        @pl.when(core_ref[0] != 0)
        def _():
            spread(give_ref, keep_ref)


def attention_backward(
    returned,
    flat,
    cot,
    resid,
    router,
    low_two,
    mixed,
    packed,
    logs,
    x,
    gain_one,
    gain_two,
    router_w,
    out_w,
    order,
    core,
    experts,
    capacity_rows,
    pieces,
    block,
):
    toks = x.shape[0]
    height = 4 * D // pieces + SMALL
    rows = block * PATCHES
    images = toks // PATCHES
    stride = returned[0].shape[0]
    slots = experts * stride

    def tile(width):
        return pl.BlockSpec((rows, width), lambda i: (i, 0))

    return pl.pallas_call(
        partial(backward_kernel, experts, capacity_rows),
        out_shape=(
            jax.ShapeDtypeStruct((toks, D), F32),
            jax.ShapeDtypeStruct((toks, 3 * D), BF16),
            jax.ShapeDtypeStruct((pieces // 2, height, D), BF16),
            jax.ShapeDtypeStruct((pieces // 2, height, D), BF16),
        ),
        in_specs=[whole((stride, D))] * experts
        + [
            tile(8),
            tile(D),
            tile(D),
            tile(LANES),
            tile(D),
            tile(D),
            tile(3 * D),
            pl.BlockSpec((block, HEADS, PATCHES), lambda i: (i, 0, 0)),
            tile(D),
            whole((1, D)),
            whole((1, D)),
            whole((D, LANES)),
            whole((D, D)),
            whole((LANES, LANES)),
            pl.BlockSpec(memory_space=pltpu.SMEM),
        ],
        out_specs=(
            tile(D),
            tile(3 * D),
            whole((pieces // 2, height, D)),
            whole((pieces // 2, height, D)),
        ),
        grid=(images // block,),
        scratch_shapes=[
            pltpu.VMEM((slots, D), BF16),
            pltpu.VMEM((slots, LANES), BF16),
            pltpu.VMEM((D, 3 * D), F32),
            pltpu.VMEM((D, D), F32),
            pltpu.VMEM((LANES, D), F32),
            pltpu.VMEM((1, D), F32),
        ],
        compiler_params=params(),
        name="attention_backward",
        cost_estimate=pl.CostEstimate(
            flops=70_000_000_000, bytes_accessed=toks * D * 20, transcendentals=0
        ),
    )(
        *returned,
        flat,
        cot,
        resid,
        router,
        low_two,
        mixed,
        packed,
        logs,
        x,
        gain_one,
        gain_two,
        router_w,
        out_w,
        order,
        core,
    )


def input_kernel(d_packed_ref, d_resid_ref, x_ref, gain_one_ref, qkv_ref, grad_ref):
    d_one = nt(d_packed_ref[...], qkv_ref[...])
    hat, inverse = standardise(x_ref[...].astype(F32))
    grad_ref[...] = d_resid_ref[...] + standardise_back(hat, inverse, gain_one_ref[...], d_one)


def input_backward(d_packed, d_resid, x, gain_one, qkv, block):
    toks = x.shape[0]
    rows = block * PATCHES

    def tile(width):
        return pl.BlockSpec((rows, width), lambda i: (i, 0))

    return pl.pallas_call(
        input_kernel,
        out_shape=jax.ShapeDtypeStruct((toks, D), F32),
        in_specs=[tile(3 * D), tile(D), tile(D), whole((1, D)), whole((D, 3 * D))],
        out_specs=tile(D),
        grid=(toks // rows,),
        compiler_params=params(),
        name="input_backward",
        cost_estimate=pl.CostEstimate(
            flops=toks * D, bytes_accessed=toks * D, transcendentals=0
        ),
    )(d_packed, d_resid, x, gain_one, qkv)


def combine_kernel(experts, rows, stride, mine_ref, flat_ref, outputs_ref, resid_ref, router_ref, block_ref):
    first, second = flat_ref[:, 0:1], flat_ref[:, 1:2]
    lane = lax.broadcasted_iota(jnp.int32, router_ref.shape, 1) * stride
    router = router_ref[...]

    def gate(flat):
        mine = (flat >= lane) & (flat < lane + stride)
        return jnp.sum(jnp.where(mine, router, 0.0), axis=1, keepdims=True)

    position = lax.broadcasted_iota(jnp.int32, (1, experts * rows), 1)
    owner = jnp.zeros_like(position)
    for e in range(1, experts):
        owner = owner + (position >= e * rows).astype(jnp.int32)
    slot = (owner ^ mine_ref[0]) * stride + (position - owner * rows)
    weight = jnp.where(slot == first, gate(first), jnp.where(slot == second, gate(second), 0.0))
    block_ref[...] = (resid_ref[...] + nn(weight.astype(BF16), outputs_ref[...])).astype(BF16)


def combine(mine, flat, outputs, resid, router, experts, stride, block):
    slots = outputs.shape[0]
    toks = resid.shape[0]
    rows = block * PATCHES

    def tile(width):
        return pl.BlockSpec((rows, width), lambda i: (i, 0))

    return pl.pallas_call(
        partial(combine_kernel, experts, slots // experts, stride),
        out_shape=jax.ShapeDtypeStruct((toks, D), BF16),
        in_specs=[
            pl.BlockSpec(memory_space=pltpu.SMEM),
            tile(8),
            whole((slots, D)),
            tile(D),
            tile(LANES),
        ],
        out_specs=tile(D),
        grid=(toks // rows,),
        compiler_params=params(),
        name="combine",
        cost_estimate=pl.CostEstimate(
            flops=toks * D, bytes_accessed=toks * D, transcendentals=0
        ),
    )(mine, flat, outputs, resid, router)


def finish_kernel(
    experts,
    core_ref,
    own_ref,
    other_ref,
    gain_one_ref,
    qkv_w_ref,
    qkv_ref,
    out_ref,
    router_ref,
    gain_two_ref,
    gain_one_grad_ref,
):
    count, height, _ = own_ref.shape
    piece = height - SMALL

    def spread(low_ref, high_ref):
        for j in range(2 * count):
            source = low_ref if j < count else high_ref
            rows = source[j % count, :piece].astype(F32)
            block, at = divmod(j * piece, D)
            if block < 3:
                qkv_ref[at : at + piece, block * D : (block + 1) * D] = rows
            else:
                out_ref[at : at + piece, :] = rows
            at = j * SMALL
            if at < experts:
                router_ref[at : at + SMALL] = source[j % count, piece:].astype(F32)
            elif at == experts:
                gain_two_ref[...] = source[j % count, piece : piece + 1].astype(F32)

    @pl.when(core_ref[0] == 0)
    def _():
        spread(own_ref, other_ref)

    @pl.when(core_ref[0] != 0)
    def _():
        spread(other_ref, own_ref)

    column = jnp.sum(qkv_ref[...] * qkv_w_ref[...].astype(F32), axis=1, keepdims=True)
    row = jnp.transpose(jnp.broadcast_to(column, (D, LANES)))[0:1]
    gain_one_grad_ref[...] = row / gain_one_ref[...]


def finish(core, own, other, gain_one, qkv, experts):
    count, height, _ = own.shape
    shapes = ((D, 3 * D), (D, D), (experts, D), (1, D), (1, D))
    return pl.pallas_call(
        partial(finish_kernel, experts),
        out_shape=tuple(jax.ShapeDtypeStruct(shape, F32) for shape in shapes),
        in_specs=[
            pl.BlockSpec(memory_space=pltpu.SMEM),
            whole((count, height, D)),
            whole((count, height, D)),
            whole((1, D)),
            whole((D, 3 * D)),
        ],
        out_specs=tuple(whole(shape) for shape in shapes),
        grid=(1,),
        compiler_params=params(),
        name="finish",
        cost_estimate=pl.CostEstimate(flops=D * D * 8, bytes_accessed=D * D * 24, transcendentals=0),
    )(core, own, other, gain_one, qkv)


SWAP = ((0, 1), (1, 0))


def spread_out(values, axes):
    return lax.all_to_all(values, axes, split_axis=0, concat_axis=0, tiled=True)


def sum_everywhere(keep, give, sums, beside, plan):
    got = lax.ppermute(give, "core", SWAP)
    pair = (keep.astype(F32) + got.astype(F32)).astype(BF16)
    sums = plan.join_grads(sums)
    pair, sums = lax.optimization_barrier((pair, sums))
    sums = plan.share_grads(sums)
    spread = spread_out(pair, plan.chips)
    spread, beside = lax.optimization_barrier((spread, beside))
    total = jnp.sum(spread.astype(F32), axis=0, keepdims=True).astype(BF16)
    total = jnp.broadcast_to(total, pair.shape)
    own = spread_out(total, plan.chips)
    return own, sums, beside


class Straight:
    def __init__(self, mesh):
        dp, expert = mesh.devices.shape
        self.devices = dp * expert
        self.sends = self.works = [range(k, k + 4) for k in range(0, expert, 4)]
        self.mesh = Mesh(mesh.devices.reshape(dp, expert // 2, 2), ("dp", "chip", "core"))
        self.everyone = ("dp", "chip", "core")
        self.owners = ("chip", "core")
        self.chips = ("dp", "chip")

    def mine(self):
        return jnp.zeros((), jnp.int32)

    def lane(self):
        return lax.axis_index(("chip", "core"))

    def place(self, expert):
        return expert

    def exchange(self, values):
        return spread_out(values, ("chip", "core"))

    def scatter(self, pieces):
        moved = self.exchange(jnp.stack(pieces))
        return [moved[k] for k in range(len(pieces))]

    def weights(self, first, second):
        return first, second

    def pass_on(self, weights, after):
        return (jnp.zeros((2,), jnp.int32), [weights[0]], [weights[1]]), after

    def start_grads(self, first, second):
        first = first.transpose(1, 0, 2).reshape(1, D, -1)
        second = second.reshape(1, -1, D)
        return lax.psum(first, "dp"), lax.psum(second, "dp")

    def join_grads(self, sums):
        return sums

    def share_grads(self, sums):
        return sums

    def end_grads(self, sums):
        return sums[0].astype(F32), sums[1].astype(F32)

    def core(self):
        return jnp.zeros((1,), jnp.int32)


class Halves:
    def __init__(self, mesh):
        self.devices = 32
        self.sends = [(1, 2, 4, 0), (7, 3, 5, 6)]
        self.works = [(0, 1, 2, 4), (3, 5, 6, 7)]
        self.mesh = Mesh(mesh.devices.reshape(2, 2, 2, 2, 2), ("y", "x", "zh", "zl", "core"))
        self.everyone = ("y", "x", "zh", "zl", "core")
        self.owners = ("zh", "zl", "core")
        self.chips = ("y", "x", "zh", "zl")
        bits = (0, 1)
        self.all = [(y, x, h, l, c) for y in bits for x in bits for h in bits for l in bits for c in bits]

    def mine(self):
        return lax.axis_index(("y", "x", "zl"))

    def lane(self):
        return jnp.zeros((), jnp.int32)

    def place(self, expert):
        low = (expert >> 1) & 1
        y = ((expert >> 2) & 1) ^ lax.axis_index("zh") ^ low
        return (4 * y + 2 * (expert & 1) + low) ^ self.mine()

    def exchange(self, values):
        return spread_out(values, ("y", "x", "zl"))

    def scatter(self, pieces):
        return [
            lax.ppermute(piece, ("y", "x", "zl"), [(i, i ^ k) for i in range(8)]) if k else piece
            for k, piece in enumerate(pieces)
        ]

    def send(self, values, route):
        pairs = []
        for source in self.all:
            target = route(*source)
            if target is not None and target != source:
                pairs.append((self.all.index(source), self.all.index(target)))
        return lax.ppermute(values, self.everyone, pairs)

    def weights(self, first, second):
        def start(core):
            def route(y, x, h, l, c):
                if c != x:
                    return None
                return (y, x, h, l, 1 - x) if y == l else (y, x, 1 - h, l, core)

            return route

        first_in = self.send(first, start(0))
        second_in = self.send(second, start(1))
        return first, second, first_in, second_in

    def pass_on(self, weights, after):
        def passed(core):
            return lambda y, x, h, l, c: (y, x, h, l, 1 - c) if y != l and c == core else None

        first, second, first_in, second_in = weights
        (first_in, second_in), after = lax.optimization_barrier(((first_in, second_in), after))
        first_on = self.send(first_in, passed(0))
        second_on = self.send(second_in, passed(1))
        y, x, low, core = (lax.axis_index(name) for name in ("y", "x", "zl", "core"))
        near = (core ^ x) & 1
        pick = jnp.stack([jnp.where(y == low, near, 1 + core), jnp.where(y == low, near, 2 - core)])
        return (pick, [first, first_in, first_on], [second, second_in, second_on]), after

    def core(self):
        return lax.axis_index("core").reshape(1)

    def start_grads(self, keep, give):
        y, x, core = (lax.axis_index(name) for name in ("y", "x", "core"))
        got = lax.ppermute(give, "core", SWAP)
        rounds = [(ry, rx) for rx in (0, 1) for ry in (0, 1)]
        picks = jnp.stack([2 * (y ^ ry) + (x ^ rx ^ core) for ry, rx in rounds])
        quarters = pair_quarters(picks, keep, got)
        sent = [
            self.send(quarter, lambda y, x, h, l, c: (y ^ ry, x ^ rx ^ c, h ^ y ^ l, l, x))
            for quarter, (ry, rx) in zip(quarters, rounds)
        ]
        return sent + [quarters[0], quarters[2]]

    def join_grads(self, pieces):
        y, x, low, core = (lax.axis_index(name) for name in ("y", "x", "zl", "core"))
        home = (y == low) & (x == core)
        turn = jnp.stack(
            [x ^ core, (home & (core == 0)).astype(jnp.int32), (home & (core == 1)).astype(jnp.int32)]
        )
        return join_quarters(turn, pieces)

    def share_grads(self, mine):
        return [mine] + [
            lax.ppermute(mine, ("y", "x"), [(i, i ^ step) for i in range(4)]) for step in (1, 2, 3)
        ]

    def end_grads(self, pieces):
        y, x = lax.axis_index("y"), lax.axis_index("x")
        return unfold((2 * y + x).reshape(1), pieces)


def shards(
    plan,
    tokens,
    gain_one,
    w_qkv,
    w_attn_out,
    gain_two,
    w_router,
    w_first,
    w_second,
    expert_ids,
    priority_ranks,
    cotangent,
):
    tok_rows = tokens.shape[0]
    experts = w_router.shape[1]
    capacity = max(2, tok_rows // experts)
    capacity_rows = -(-capacity // 16) * 16
    stride = capacity_rows + EXTRA
    gain_one = gain_one.reshape(1, D)
    gain_two = gain_two.reshape(1, D)
    places = plan.place(jnp.arange(experts, dtype=jnp.int32))
    order = (places[:, None] == jnp.arange(LANES, dtype=jnp.int32)).astype(BF16)
    router_w = jnp.dot(w_router, order, preferred_element_type=F32).astype(BF16)
    order = jnp.pad(order, ((0, LANES - experts), (0, 0)))

    mine = plan.mine().reshape(1)
    lane = plan.lane().reshape(1)

    weights = plan.weights(w_first, w_second)
    flat, flat_cols = route(plan.place(expert_ids.T), priority_ranks, experts, capacity, stride)
    grad_rows = plan.exchange(dispatch_grad(mine, flat, cotangent, experts, capacity_rows, stride))
    packed, logs, mixed, resid, low_two, router = attention_forward(
        tokens, gain_one, w_qkv, w_attn_out, gain_two, router_w, experts, 4
    )
    pieces = [None] * experts
    for steps in plan.sends:
        some = dispatch(flat, low_two, steps, capacity_rows, stride)
        flat, some = lax.optimization_barrier((flat, some))
        for k, piece in zip(steps, some):
            pieces[k] = piece
    weights, pieces[0] = plan.pass_on(weights, pieces[0])
    received = plan.scatter(pieces)
    back = [None] * experts
    kept = ()
    at = 0
    for steps in plan.works:
        sources = jnp.asarray(steps, jnp.int32) ^ mine
        some, kept = expert_apply(
            at,
            sources,
            lane,
            [received[k] for k in steps],
            grad_rows,
            weights,
            router_w,
            experts,
            stride,
            kept,
        )
        at += len(steps)
        for k, piece in zip(steps, some):
            back[k] = piece
    outputs, hidden, d_pre, d_out, low = kept
    returned = plan.scatter(back)
    early = [returned[k] for k in plan.works[0]]
    low, early = lax.optimization_barrier((low, early))
    for k, piece in zip(plan.works[0], early):
        returned[k] = piece
    keep, give = expert_grads(plan.core(), low, d_out, hidden, d_pre)
    returned, keep, give, outputs = lax.optimization_barrier((returned, keep, give, outputs))
    outputs = plan.exchange(outputs)
    sums = plan.start_grads(keep, give)
    core = lax.axis_index("core").reshape(1)
    d_resid, d_packed, keep, give = attention_backward(
        returned,
        flat_cols,
        cotangent,
        resid,
        router,
        low_two,
        mixed,
        packed,
        logs,
        tokens,
        gain_one,
        gain_two,
        router_w,
        w_attn_out,
        order,
        core,
        experts,
        capacity_rows,
        plan.devices,
        4,
    )
    keep, give, d_packed, outputs, sums = lax.optimization_barrier(
        (keep, give, d_packed, outputs, sums)
    )
    grad_tokens = input_backward(d_packed, d_resid, tokens, gain_one, w_qkv, 4)
    outputs = outputs.reshape(experts * capacity_rows, D)
    block_out = combine(mine, flat_cols, outputs, resid, router, experts, stride, 4)
    own, sums, beside = sum_everywhere(keep, give, sums, (grad_tokens, block_out), plan)
    grad_tokens, block_out = beside
    first_grad, second_grad = plan.end_grads(sums)
    own, first_grad, second_grad = lax.optimization_barrier((own, first_grad, second_grad))
    other = lax.ppermute(own, "core", SWAP)
    qkv_grad, out_grad, router_grad, gain_two_grad, gain_one_grad = finish(
        core, own, other, gain_one, w_qkv, experts
    )
    return (
        block_out,
        grad_tokens,
        gain_one_grad.reshape(D),
        qkv_grad,
        out_grad,
        gain_two_grad.reshape(D),
        router_grad.T,
        first_grad,
        second_grad,
    )


def solution(mesh):
    plan = Halves(mesh) if mesh.devices.shape == (4, 8) else Straight(mesh)
    both = P(plan.everyone, None)
    one = P(plan.owners, None, None)
    in_specs = (both, P(), P(), P(), P(), P(), one, one, both, both, both)
    out_specs = (both, both, P(), P(), P(), P(), P(), one, one)
    return jax.shard_map(
        partial(shards, plan),
        mesh=plan.mesh,
        in_specs=in_specs,
        out_specs=out_specs,
        check_vma=False,
    )
```

profile of v0, /device:TPU:0, one launch (start us, length us, event | category | flops | bytes accessed | tf_op | source)
XLA Modules:
  0.0 351.6 jit_solution(10382647492445480515)
XLA Ops:
  0.7 3.7 %collective-permute-start.4 = (bf16[1,512,2048]{2,1,0:T(8,128)(2,1)}, bf16[1,512,2048]{2,1,0:T(8,128)(2,1)}, u32[]{:S(2)}, u32[]{:S(2)}) collective-permute-start(bf16[1,512,2048]{2,1,0:T(8,128)(2,1)} %refs_6_.3), channel_id=1, source_target_pairs={{0,1},{2,6},{4,5},{6,2},{9,8},{11,14},{13,12},{15,10},{16,20},{18,... | collective-permute-start | bytes 6291464 | tf_op jit(solution)/shard_map/ppermute | solution.py:1050
  8.3 4.1 %route.1 = (s32[8,2304]{1,0:T(8,128)}, s32[2304,8]{1,0:T(8,128)}) custom-call(s32[2,2304]{1,0:T(2,128)} %fusion.2.ids_ref, s32[1,2304]{1,0:T(1,128)} %ranks_ref.1), custom_call_target="tpu_custom_call" | custom-call | flops 1358954496 | bytes 110592 | tf_op jit(solution)/shard_map/route/pallas_call | solution.py:96
  12.4 10.3 %dispatch_grad.1 = bf16[8,288,512]{2,1,0:T(8,128)(2,1)} custom-call(s32[1]{0:T(128)} %bitcast.8.mine_ref, s32[8,2304]{1,0:T(8,128)} %get-tuple-element.112.flat_ref, f32[2304,512]{1,0:T(8,128)} %refs_9_.5), custom_call_target="tpu_custom_call" | custom-call | flops 10871635968 | bytes 7077888 | tf_op jit(solution)/shard_map/dispatch_grad/pallas_call | solution.py:133
  22.8 5.2 %all-to-all-start = ((bf16[8,288,512]{2,1,0:T(8,128)(2,1)}), bf16[8,288,512]{2,1,0:T(8,128)(2,1)S(1)}, u32[]{:S(2)}, u32[]{:S(2)}) async-start(bf16[8,288,512]{2,1,0:T(8,128)(2,1)} %dispatch_grad.1), calls=%async_computation | async-start | bytes 4718592 | tf_op jit(solution)/shard_map/all_to_all | solution.py:945
  28.9 24.5 %attention_forward.1 = (bf16[2304,1536]{1,0:T(8,128)(2,1)}, f32[16,8,144]{2,1,0:T(8,128)}, bf16[2304,512]{1,0:T(8,128)(2,1)}, f32[2304,512]{1,0:T(8,128)}, bf16[...) custom-call(bf16[2304,512]{1,0:T(8,128)(2,1)} %x_ref.3, f32[1,512]{1,0:T(1,128)} %bitcast.37, bf16[512,1536]{1,0:T(8,128)(2,1)} %qkv_w_ref.1, ...), custom_call_target="tpu_custom_call" | custom-call | flops 31000000512 | bytes 23592960 | tf_op jit(solution)/shard_map/attention_forward/pallas_call | solution.py:250
  53.4 5.3 %dispatch.2 = (bf16[288,512]{1,0:T(8,128)(2,1)}, bf16[288,512]{1,0:T(8,128)(2,1)}, bf16[288,512]{1,0:T(8,128)(2,1)}, bf16[288,512]{1,0:T(8,128)(2,1)}) custom-call(s32[8,2304]{1,0:T(8,128)} %get-tuple-element.112.flat_ref, bf16[2304,512]{1,0:T(8,128)(2,1)} %get-tuple-element.107.low_ref.refs_12_), custom_call_target="tpu_custom_call" | custom-call | flops 5435817984 | bytes 4718592 | tf_op jit(solution)/shard_map/dispatch/pallas_call | solution.py:156
  63.0 8.3 %collective-permute-start.10 = (bf16[288,512]{1,0:T(8,128)(2,1)}, bf16[288,512]{1,0:T(8,128)(2,1)S(1)}, u32[]{:S(2)}, u32[]{:S(2)}) collective-permute-start(bf16[288,512]{1,0:T(8,128)(2,1)} %get-tuple-element.127), channel_id=1, source_target_pairs={{0,16},{2,18},{8,24},{10,26},{16,0},{18,2},{24,8},{26,10},{1,17},{... | collective-permute-start | bytes 884744 | tf_op jit(solution)/shard_map/ppermute | solution.py:1040
  73.6 5.4 %dispatch.3 = (bf16[288,512]{1,0:T(8,128)(2,1)}, bf16[288,512]{1,0:T(8,128)(2,1)}, bf16[288,512]{1,0:T(8,128)(2,1)}, bf16[288,512]{1,0:T(8,128)(2,1)}) custom-call(s32[8,2304]{1,0:T(8,128)} %get-tuple-element.112.flat_ref, bf16[2304,512]{1,0:T(8,128)(2,1)} %get-tuple-element.107.low_ref.refs_12_), custom_call_target="tpu_custom_call" | custom-call | flops 5435817984 | bytes 4718592 | tf_op jit(solution)/shard_map/dispatch/pallas_call | solution.py:156
  80.7 4.0 %collective-permute-done.10.refs_3_ = bf16[288,512]{1,0:T(8,128)(2,1)S(1)} collective-permute-done((bf16[288,512]{1,0:T(8,128)(2,1)}, bf16[288,512]{1,0:T(8,128)(2,1)S(1)}, u32[]{:S(2)}, u32[]{:S(2)}) %collective-permute-start.10) | collective-permute-done | bytes 294944 | tf_op jit(solution)/shard_map/ppermute | solution.py:1040
  85.0 3.5 %collective-permute-start.1 = (bf16[288,512]{1,0:T(8,128)(2,1)}, bf16[288,512]{1,0:T(8,128)(2,1)}, u32[]{:S(2)}, u32[]{:S(2)}) collective-permute-start(bf16[288,512]{1,0:T(8,128)(2,1)} %get-tuple-element.118), channel_id=1, source_target_pairs={{0,18},{2,16},{8,26},{10,24},{16,2},{18,0},{24,10},{26,8},{1,19},{... | collective-permute-start | bytes 884744 | tf_op jit(solution)/shard_map/ppermute | solution.py:1040
  92.0 19.8 %expert_apply.2 = (bf16[304,512]{1,0:T(8,128)(2,1)}, bf16[304,512]{1,0:T(8,128)(2,1)}, bf16[304,512]{1,0:T(8,128)(2,1)}, bf16[304,512]{1,0:T(8,128)(2,1)}, bf16[...) custom-call(s32[4]{0:T(128)} %broadcast_xor_fusion.sources_ref, ...), custom_call_target="tpu_custom_call" | custom-call | flops 18119393280 | bytes 9437184 | tf_op jit(solution)/shard_map/expert_apply/pallas_call | solution.py:392
  116.0 19.8 %expert_apply.3 = (bf16[304,512]{1,0:T(8,128)(2,1)}, bf16[304,512]{1,0:T(8,128)(2,1)}, bf16[304,512]{1,0:T(8,128)(2,1)}, bf16[304,512]{1,0:T(8,128)(2,1)}, bf16[...) custom-call(s32[4]{0:T(128)} %broadcast_xor_fusion.1.sources_ref, ...), custom_call_target="tpu_custom_call", output_to_operand_aliasing={{4}: (15, {}), {5}: (16, {}), {6}: (17, {}), {7}: (18, {}),... | custom-call | flops 18119393280 | bytes 9437184 | tf_op jit(solution)/shard_map/expert_apply/pallas_call | solution.py:392
  136.9 2.9 collective-permute-start.15
  142.1 15.9 %expert_grads.1 = (bf16[4,512,512]{2,1,0:T(8,128)(2,1)}, bf16[4,512,512]{2,1,0:T(8,128)(2,1)}) custom-call(s32[1]{0:T(128)} %bitcast.9.core_ref.refs_22_, bf16[2304,512]{1,0:T(8,128)(2,1)} %get-tuple-element.146.low_ref, bf16[2304,512]{1,0:T(8,128)(2,1)} %get-tuple-element.147.d_out_ref, bf16[2304,2048]{1,0:T(8,128)(2,1)} %get-tuple-element.148.hidden_ref, ...), custom_call_target="tpu_custom_call" | custom-call | flops 19327352832 | bytes 18874368 | tf_op jit(solution)/shard_map/expert_grads/pallas_call | solution.py:440
  158.8 3.0 collective-permute-done.16.refs_6_
  163.2 3.6 %all-to-all-start.1 = ((bf16[8,288,512]{2,1,0:T(8,128)(2,1)}), bf16[8,288,512]{2,1,0:T(8,128)(2,1)S(1)}, u32[]{:S(2)}, u32[]{:S(2)}) async-start(bf16[8,288,512]{2,1,0:T(8,128)(2,1)} %get-tuple-element.170), calls=%async_computation.1 | async-start | bytes 4718592 | tf_op jit(solution)/shard_map/all_to_all | solution.py:945
  166.8 5.4 %pair_quarters.1 = (bf16[512,512]{1,0:T(8,128)(2,1)}, bf16[512,512]{1,0:T(8,128)(2,1)}, bf16[512,512]{1,0:T(8,128)(2,1)}, bf16[512,512]{1,0:T(8,128)(2,1)}) custom-call(s32[4]{0:T(128)} %pad_add_fusion.1.picks_ref, bf16[4,512,512]{2,1,0:T(8,128)(2,1)} %get-tuple-element.171.keep_ref, bf16[4,512,512]{2,1,0:T(8,128)(2,1)} %collective-permute-done.18.got_ref), custom_call_target="tpu_custom_call" | custom-call | flops 262144 | bytes 6291456 | tf_op jit(solution)/shard_map/pair_quarters/pallas_call | solution.py:472
  172.9 6.0 %collective-permute-start.20 = (bf16[512,512]{1,0:T(8,128)(2,1)}, bf16[512,512]{1,0:T(8,128)(2,1)}, u32[]{:S(2)}, u32[]{:S(2)}) collective-permute-start(bf16[512,512]{1,0:T(8,128)(2,1)} %get-tuple-element.174), channel_id=1, source_target_pairs={{0,16},{1,24},{2,22},{3,30},{4,20},{5,28},{6,18},{7,26},{8,25},{9,... | collective-permute-start | bytes 1572872 | tf_op jit(solution)/shard_map/ppermute | solution.py:1050
  178.9 2.9 collective-permute-start.21
  182.6 67.4 %attention_backward.1 = (f32[2304,512]{1,0:T(8,128)}, bf16[2304,1536]{1,0:T(8,128)(2,1)}, bf16[16,72,512]{2,1,0:T(8,128)(2,1)}, bf16[16,72,512]{2,1,0:T(8,128)(2,1)}) custom-call(bf16[304,512]{1,0:T(8,128)(2,1)} %get-tuple-element.153.refs_0_, bf16[304,512]{1,0:T(8,128)(2,1)} %copy-done.10, bf16[304,512]{1,0:T(8,128)(2,1)} %copy-done.11, ...), custom_call_target="tpu_custom_call" | custom-call | flops 70000001024 | bytes 23592960 | tf_op jit(solution)/shard_map/attention_backward/pallas_call | solution.py:737
  251.7 3.7 %join_quarters.1.refs_0_ = bf16[2,512,512]{2,1,0:T(8,128)(2,1)} custom-call(s32[3]{0:T(128)} %pad_add_fusion.2.turn_ref, bf16[512,512]{1,0:T(8,128)(2,1)} %copy-done.7, bf16[512,512]{1,0:T(8,128)(2,1)} %collective-permute-done.20.b_ref, bf16[512,512]{1,0:T(8,128)(2,1)} %collective-permute-done.21.c_ref, bf16[512,512]{1,0:T(8,128)(2,1)} %collective-permute-done.22.d_ref, ...), custom_call_target="tpu_custom_call" | custom-call | flops 262144 | bytes 3145728 | tf_op jit(solution)/shard_map/join_quarters/pallas_call | solution.py:508
  255.4 2.6 add_convert_fusion
  258.0 6.0 %all-to-all-start.2 = ((bf16[16,72,512]{2,1,0:T(8,128)(2,1)}), bf16[16,72,512]{2,1,0:T(8,128)(2,1)S(1)}, u32[]{:S(2)}, u32[]{:S(2)}) async-start(bf16[16,72,512]{2,1,0:T(8,128)(2,1)} %add_convert_fusion), calls=%async_computation.2 | async-start | bytes 2359296 | tf_op jit(solution)/shard_map/all_to_all | solution.py:945
  267.6 12.8 %combine.1 = bf16[2304,512]{1,0:T(8,128)(2,1)} custom-call(s32[1]{0:T(128)} %bitcast.8.mine_ref, s32[2304,8]{1,0:T(8,128)} %get-tuple-element.161.refs_8_.flat_ref, bf16[2304,512]{1,0:T(8,128)(2,1)} %bitcast.36, f32[2304,512]{1,0:T(8,128)} %get-tuple-element.162.refs_10_.resid_ref, f32[2304,128]{1,0:T(8,128)} %get-tuple-element.163.refs_11_.router_ref), custom_call_target="tpu_custom_call" | custom-call | flops 1179648 | bytes 1179648 | tf_op jit(solution)/shard_map/combine/pallas_call | solution.py:856
  280.4 10.8 %input_backward.1 = f32[2304,512]{1,0:T(8,128)} custom-call(bf16[2304,1536]{1,0:T(8,128)(2,1)} %get-tuple-element.186.d_packed_ref, f32[2304,512]{1,0:T(8,128)} %get-tuple-element.187.d_resid_ref, bf16[2304,512]{1,0:T(8,128)(2,1)} %x_ref.3, f32[1,512]{1,0:T(1,128)} %bitcast.39, bf16[512,1536]{1,0:T(8,128)(2,1)} %qkv_w_ref.1), custom_call_target="tpu_custom_call" | custom-call | flops 1179648 | bytes 1179648 | tf_op jit(solution)/shard_map/input_backward/pallas_call | solution.py:816
  291.2 3.8 %all-to-all-done.2 = bf16[16,72,512]{2,1,0:T(8,128)(2,1)S(1)} async-done(((bf16[16,72,512]{2,1,0:T(8,128)(2,1)}), bf16[16,72,512]{2,1,0:T(8,128)(2,1)S(1)}, u32[]{:S(2)}, u32[]{:S(2)}) %all-to-all-start.2) | async-done | bytes 1179680 | tf_op jit(solution)/shard_map/all_to_all | solution.py:945
  296.2 3.7 %all-to-all-start.3 = ((bf16[16,72,512]{2,1,0:T(8,128)(2,1)}), bf16[16,72,512]{2,1,0:T(8,128)(2,1)S(1)}, u32[]{:S(2)}, u32[]{:S(2)}) async-start(bf16[16,72,512]{2,1,0:T(8,128)(2,1)} %broadcast_in_dim.2), calls=%async_computation.3 | async-start | bytes 2359296 | tf_op jit(solution)/shard_map/all_to_all | solution.py:945
  299.9 4.0 %collective-permute-done.24.refs_1_ = bf16[2,512,512]{2,1,0:T(8,128)(2,1)S(1)} collective-permute-done((bf16[2,512,512]{2,1,0:T(8,128)(2,1)}, bf16[2,512,512]{2,1,0:T(8,128)(2,1)S(1)}, u32[]{:S(2)}, u32[]{:S(2)}) %collective-permute-start.24) | collective-permute-done | bytes 1048608 | tf_op jit(solution)/shard_map/ppermute | solution.py:1103
  303.9 33.3 %collective-permute-done.26.refs_3_ = bf16[2,512,512]{2,1,0:T(8,128)(2,1)} collective-permute-done((bf16[2,512,512]{2,1,0:T(8,128)(2,1)}, bf16[2,512,512]{2,1,0:T(8,128)(2,1)}, u32[]{:S(2)}, u32[]{:S(2)}) %collective-permute-start.26) | collective-permute-done | bytes 1048608 | tf_op jit(solution)/shard_map/ppermute | solution.py:1103
  337.2 5.8 %unfold.1 = (f32[1,512,2048]{2,1,0:T(8,128)}, f32[1,2048,512]{2,1,0:T(8,128)}) custom-call(s32[1]{0:T(128)} %bitcast.18.corner_ref, bf16[2,512,512]{2,1,0:T(8,128)(2,1)} %join_quarters.1.refs_0_, bf16[2,512,512]{2,1,0:T(8,128)(2,1)} %copy-done.8, bf16[2,512,512]{2,1,0:T(8,128)(2,1)} %copy-done.9, bf16[2,512,512]{2,1,0:T(8,128)(2,1)} %collective-permute-done.26.refs_3_), custom_call_target="tpu_custom_call" | custom-call | flops 104857600000 | bytes 12582912 | tf_op jit(solution)/shard_map/unfold/pallas_call | solution.py:532
  343.1 2.8 collective-permute-done.27.other_ref
  346.9 4.4 %finish.1 = (f32[512,1536]{1,0:T(8,128)}, f32[512,512]{1,0:T(8,128)}, f32[8,512]{1,0:T(8,128)}, f32[1,512]{1,0:T(1,128)}, f32[1,512]{1,0:T(1,128)}) custom-call(s32[1]{0:T(128)} %bitcast.9.core_ref.refs_22_, bf16[16,72,512]{2,1,0:T(8,128)(2,1)} %copy-done.3, bf16[16,72,512]{2,1,0:T(8,128)(2,1)} %copy-done.6, f32[1,512]{1,0:T(1,128)} %bitcast.40, ...), custom_call_target="tpu_custom_call" | custom-call | flops 2097152 | bytes 6291456 | tf_op jit(solution)/shard_map/finish/pallas_call | solution.py:923
  (104 shorter events, 35.8 us)
Async XLA Ops:
  0.7 58.1 %collective-permute-start.4 = (bf16[1,512,2048]{2,1,0:T(8,128)(2,1)}, bf16[1,512,2048]{2,1,0:T(8,128)(2,1)}, u32[]{:S(2)}, u32[]{:S(2)}) collective-permute-start(bf16[1,512,2048]{2,1,0:T(8,128)(2,1)} %refs_6_.3), channel_id=1, source_target_pairs={{0,1},{2,6},{4,5},{6,2},{9,8},{11,14},{13,12},{15,10},{16,20},{18,... | collective-permute-start | bytes 6291464 | tf_op jit(solution)/shard_map/ppermute | solution.py:1050
  4.4 54.4 %collective-permute-start.5 = (bf16[1,2048,512]{2,1,0:T(8,128)(2,1)}, bf16[1,2048,512]{2,1,0:T(8,128)(2,1)}, u32[]{:S(2)}, u32[]{:S(2)}) collective-permute-start(bf16[1,2048,512]{2,1,0:T(8,128)(2,1)} %refs_9_.4), channel_id=1, source_target_pairs={{0,1},{2,7},{4,5},{6,3},{9,8},{11,15},{13,12},{15,11},{16,21},{18,... | collective-permute-start | bytes 6291464 | tf_op jit(solution)/shard_map/ppermute | solution.py:1050
  22.8 67.8 %all-to-all-start = ((bf16[8,288,512]{2,1,0:T(8,128)(2,1)}), bf16[8,288,512]{2,1,0:T(8,128)(2,1)S(1)}, u32[]{:S(2)}, u32[]{:S(2)}) async-start(bf16[8,288,512]{2,1,0:T(8,128)(2,1)} %dispatch_grad.1), calls=%async_computation | async-start | bytes 4718592 | tf_op jit(solution)/shard_map/all_to_all | solution.py:945
  58.8 30.3 %collective-permute-start.6 = (bf16[1,512,2048]{2,1,0:T(8,128)(2,1)}, bf16[1,512,2048]{2,1,0:T(8,128)(2,1)}, u32[]{:S(2)}, u32[]{:S(2)}) collective-permute-start(bf16[1,512,2048]{2,1,0:T(8,128)(2,1)} %collective-permute-done.4.refs_7_), channel_id=1, source_target_pairs={{2,3},{6,7},{10,11},{14,15},{16,17},{20,21},{24,25},{28,29}} | collective-permute-start | bytes 6291464 | tf_op jit(solution)/shard_map/ppermute | solution.py:1050
  60.7 29.8 %collective-permute-start.7 = (bf16[1,2048,512]{2,1,0:T(8,128)(2,1)}, bf16[1,2048,512]{2,1,0:T(8,128)(2,1)}, u32[]{:S(2)}, u32[]{:S(2)}) collective-permute-start(bf16[1,2048,512]{2,1,0:T(8,128)(2,1)} %collective-permute-done.5.refs_10_), channel_id=1, source_target_pairs={{3,2},{7,6},{11,10},{15,14},{17,16},{21,20},{25,24},{29,28}} | collective-permute-start | bytes 6291464 | tf_op jit(solution)/shard_map/ppermute | solution.py:1050
  63.0 21.6 %collective-permute-start.10 = (bf16[288,512]{1,0:T(8,128)(2,1)}, bf16[288,512]{1,0:T(8,128)(2,1)S(1)}, u32[]{:S(2)}, u32[]{:S(2)}) collective-permute-start(bf16[288,512]{1,0:T(8,128)(2,1)} %get-tuple-element.127), channel_id=1, source_target_pairs={{0,16},{2,18},{8,24},{10,26},{16,0},{18,2},{24,8},{26,10},{1,17},{... | collective-permute-start | bytes 884744 | tf_op jit(solution)/shard_map/ppermute | solution.py:1040
  71.3 13.7 %collective-permute-start.8 = (bf16[288,512]{1,0:T(8,128)(2,1)}, bf16[288,512]{1,0:T(8,128)(2,1)S(1)}, u32[]{:S(2)}, u32[]{:S(2)}) collective-permute-start(bf16[288,512]{1,0:T(8,128)(2,1)} %get-tuple-element.125), channel_id=1, source_target_pairs={{0,2},{2,0},{8,10},{10,8},{16,18},{18,16},{24,26},{26,24},{1,3},{3... | collective-permute-start | bytes 884744 | tf_op jit(solution)/shard_map/ppermute | solution.py:1040
  72.6 15.8 %collective-permute-start.9 = (bf16[288,512]{1,0:T(8,128)(2,1)}, bf16[288,512]{1,0:T(8,128)(2,1)}, u32[]{:S(2)}, u32[]{:S(2)}) collective-permute-start(bf16[288,512]{1,0:T(8,128)(2,1)} %get-tuple-element.126), channel_id=1, source_target_pairs={{0,8},{2,10},{8,0},{10,2},{16,24},{18,26},{24,16},{26,18},{1,9},{3... | collective-permute-start | bytes 884744 | tf_op jit(solution)/shard_map/ppermute | solution.py:1040
  84.7 29.5 %collective-permute-start = (bf16[288,512]{1,0:T(8,128)(2,1)}, bf16[288,512]{1,0:T(8,128)(2,1)S(1)}, u32[]{:S(2)}, u32[]{:S(2)}) collective-permute-start(bf16[288,512]{1,0:T(8,128)(2,1)} %get-tuple-element.117), channel_id=1, source_target_pairs={{0,10},{2,8},{8,2},{10,0},{16,26},{18,24},{24,18},{26,16},{1,11},{... | collective-permute-start | bytes 884744 | tf_op jit(solution)/shard_map/ppermute | solution.py:1040
  85.0 29.9 %collective-permute-start.1 = (bf16[288,512]{1,0:T(8,128)(2,1)}, bf16[288,512]{1,0:T(8,128)(2,1)}, u32[]{:S(2)}, u32[]{:S(2)}) collective-permute-start(bf16[288,512]{1,0:T(8,128)(2,1)} %get-tuple-element.118), channel_id=1, source_target_pairs={{0,18},{2,16},{8,26},{10,24},{16,2},{18,0},{24,10},{26,8},{1,19},{... | collective-permute-start | bytes 884744 | tf_op jit(solution)/shard_map/ppermute | solution.py:1040
  88.5 27.5 %collective-permute-start.2 = (bf16[288,512]{1,0:T(8,128)(2,1)}, bf16[288,512]{1,0:T(8,128)(2,1)}, u32[]{:S(2)}, u32[]{:S(2)}) collective-permute-start(bf16[288,512]{1,0:T(8,128)(2,1)} %get-tuple-element.119), channel_id=1, source_target_pairs={{0,24},{2,26},{8,16},{10,18},{16,8},{18,10},{24,0},{26,2},{1,25},{... | collective-permute-start | bytes 884744 | tf_op jit(solution)/shard_map/ppermute | solution.py:1040
  89.1 27.0 %collective-permute-start.3 = (bf16[288,512]{1,0:T(8,128)(2,1)}, bf16[288,512]{1,0:T(8,128)(2,1)}, u32[]{:S(2)}, u32[]{:S(2)}) collective-permute-start(bf16[288,512]{1,0:T(8,128)(2,1)} %get-tuple-element.120), channel_id=1, source_target_pairs={{0,26},{2,24},{8,18},{10,16},{16,10},{18,8},{24,2},{26,0},{1,27},{... | collective-permute-start | bytes 884744 | tf_op jit(solution)/shard_map/ppermute | solution.py:1040
  111.8 27.9 %collective-permute-start.11 = (bf16[304,512]{1,0:T(8,128)(2,1)}, bf16[304,512]{1,0:T(8,128)(2,1)S(1)}, u32[]{:S(2)}, u32[]{:S(2)}) collective-permute-start(bf16[304,512]{1,0:T(8,128)(2,1)} %get-tuple-element.135), channel_id=1, source_target_pairs={{0,2},{2,0},{8,10},{10,8},{16,18},{18,16},{24,26},{26,24},{1,3},{3... | collective-permute-start | bytes 933896 | tf_op jit(solution)/shard_map/ppermute | solution.py:1040
  114.9 25.4 %collective-permute-start.12 = (bf16[304,512]{1,0:T(8,128)(2,1)}, bf16[304,512]{1,0:T(8,128)(2,1)S(1)}, u32[]{:S(2)}, u32[]{:S(2)}) collective-permute-start(bf16[304,512]{1,0:T(8,128)(2,1)} %get-tuple-element.136), channel_id=1, source_target_pairs={{0,8},{2,10},{8,0},{10,2},{16,24},{18,26},{24,16},{26,18},{1,9},{3... | collective-permute-start | bytes 933896 | tf_op jit(solution)/shard_map/ppermute | solution.py:1040
  114.9 27.2 %collective-permute-start.13 = (bf16[304,512]{1,0:T(8,128)(2,1)}, bf16[304,512]{1,0:T(8,128)(2,1)S(1)}, u32[]{:S(2)}, u32[]{:S(2)}) collective-permute-start(bf16[304,512]{1,0:T(8,128)(2,1)} %get-tuple-element.137), channel_id=1, source_target_pairs={{0,16},{2,18},{8,24},{10,26},{16,0},{18,2},{24,8},{26,10},{1,17},{... | collective-permute-start | bytes 933896 | tf_op jit(solution)/shard_map/ppermute | solution.py:1040
  135.8 22.2 %collective-permute-start.14 = (bf16[304,512]{1,0:T(8,128)(2,1)}, bf16[304,512]{1,0:T(8,128)(2,1)S(1)}, u32[]{:S(2)}, u32[]{:S(2)}) collective-permute-start(bf16[304,512]{1,0:T(8,128)(2,1)} %get-tuple-element.141), channel_id=1, source_target_pairs={{0,10},{2,8},{8,2},{10,0},{16,26},{18,24},{24,18},{26,16},{1,11},{... | collective-permute-start | bytes 933896 | tf_op jit(solution)/shard_map/ppermute | solution.py:1040
  136.9 21.9 %collective-permute-start.15 = (bf16[304,512]{1,0:T(8,128)(2,1)}, bf16[304,512]{1,0:T(8,128)(2,1)S(1)}, u32[]{:S(2)}, u32[]{:S(2)}) collective-permute-start(bf16[304,512]{1,0:T(8,128)(2,1)} %get-tuple-element.143), channel_id=1, source_target_pairs={{0,18},{2,16},{8,26},{10,24},{16,2},{18,0},{24,10},{26,8},{1,19},{... | collective-permute-start | bytes 933896 | tf_op jit(solution)/shard_map/ppermute | solution.py:1040
  139.7 22.1 %collective-permute-start.16 = (bf16[304,512]{1,0:T(8,128)(2,1)}, bf16[304,512]{1,0:T(8,128)(2,1)S(1)}, u32[]{:S(2)}, u32[]{:S(2)}) collective-permute-start(bf16[304,512]{1,0:T(8,128)(2,1)} %get-tuple-element.144), channel_id=1, source_target_pairs={{0,24},{2,26},{8,16},{10,18},{16,8},{18,10},{24,0},{26,2},{1,25},{... | collective-permute-start | bytes 933896 | tf_op jit(solution)/shard_map/ppermute | solution.py:1040
  140.3 21.5 %collective-permute-start.17 = (bf16[304,512]{1,0:T(8,128)(2,1)}, bf16[304,512]{1,0:T(8,128)(2,1)S(1)}, u32[]{:S(2)}, u32[]{:S(2)}) collective-permute-start(bf16[304,512]{1,0:T(8,128)(2,1)} %get-tuple-element.145), channel_id=1, source_target_pairs={{0,26},{2,24},{8,18},{10,16},{16,10},{18,8},{24,2},{26,0},{1,27},{... | collective-permute-start | bytes 933896 | tf_op jit(solution)/shard_map/ppermute | solution.py:1040
  161.8 5.0 %collective-permute-start.18 = (bf16[4,512,512]{2,1,0:T(8,128)(2,1)}, bf16[4,512,512]{2,1,0:T(8,128)(2,1)}, u32[]{:S(2)}, u32[]{:S(2)}) collective-permute-start(bf16[4,512,512]{2,1,0:T(8,128)(2,1)} %get-tuple-element.172), channel_id=1, source_target_pairs={{0,1},{1,0},{2,3},{3,2},{4,5},{5,4},{6,7},{7,6},{8,9},{9,8},{10,11... | collective-permute-start | bytes 6291464 | tf_op jit(solution)/shard_map/ppermute | solution.py:1083
  163.2 87.7 %all-to-all-start.1 = ((bf16[8,288,512]{2,1,0:T(8,128)(2,1)}), bf16[8,288,512]{2,1,0:T(8,128)(2,1)S(1)}, u32[]{:S(2)}, u32[]{:S(2)}) async-start(bf16[8,288,512]{2,1,0:T(8,128)(2,1)} %get-tuple-element.170), calls=%async_computation.1 | async-start | bytes 4718592 | tf_op jit(solution)/shard_map/all_to_all | solution.py:945
  172.2 77.9 %collective-permute-start.19 = (bf16[512,512]{1,0:T(8,128)(2,1)}, bf16[512,512]{1,0:T(8,128)(2,1)S(1)}, u32[]{:S(2)}, u32[]{:S(2)}) collective-permute-start(bf16[512,512]{1,0:T(8,128)(2,1)} %get-tuple-element.183.own_a_ref), channel_id=1, source_target_pairs={{1,8},{2,6},{3,14},{5,12},{6,2},{7,10},{8,9},{9,1},{10,15},{11,7},... | collective-permute-start | bytes 1572872 | tf_op jit(solution)/shard_map/ppermute | solution.py:1050
  172.9 77.2 %collective-permute-start.20 = (bf16[512,512]{1,0:T(8,128)(2,1)}, bf16[512,512]{1,0:T(8,128)(2,1)}, u32[]{:S(2)}, u32[]{:S(2)}) collective-permute-start(bf16[512,512]{1,0:T(8,128)(2,1)} %get-tuple-element.174), channel_id=1, source_target_pairs={{0,16},{1,24},{2,22},{3,30},{4,20},{5,28},{6,18},{7,26},{8,25},{9,... | collective-permute-start | bytes 1572872 | tf_op jit(solution)/shard_map/ppermute | solution.py:1050
  178.9 71.3 %collective-permute-start.21 = (bf16[512,512]{1,0:T(8,128)(2,1)}, bf16[512,512]{1,0:T(8,128)(2,1)}, u32[]{:S(2)}, u32[]{:S(2)}) collective-permute-start(bf16[512,512]{1,0:T(8,128)(2,1)} %get-tuple-element.184.own_c_ref), channel_id=1, source_target_pairs={{0,8},{1,0},{2,14},{3,6},{4,12},{5,4},{6,10},{7,2},{8,1},{10,7},{1... | collective-permute-start | bytes 1572872 | tf_op jit(solution)/shard_map/ppermute | solution.py:1050
  181.7 69.2 %collective-permute-start.22 = (bf16[512,512]{1,0:T(8,128)(2,1)}, bf16[512,512]{1,0:T(8,128)(2,1)}, u32[]{:S(2)}, u32[]{:S(2)}) collective-permute-start(bf16[512,512]{1,0:T(8,128)(2,1)} %get-tuple-element.176), channel_id=1, source_target_pairs={{0,24},{1,16},{2,30},{3,22},{4,28},{5,20},{6,26},{7,18},{8,17},{9,... | collective-permute-start | bytes 1572872 | tf_op jit(solution)/shard_map/ppermute | solution.py:1050
  250.9 4.5 %collective-permute-start.23 = (bf16[16,72,512]{2,1,0:T(8,128)(2,1)}, bf16[16,72,512]{2,1,0:T(8,128)(2,1)}, u32[]{:S(2)}, u32[]{:S(2)}) collective-permute-start(bf16[16,72,512]{2,1,0:T(8,128)(2,1)} %get-tuple-element.178), channel_id=1, source_target_pairs={{0,1},{1,0},{2,3},{3,2},{4,5},{5,4},{6,7},{7,6},{8,9},{9,8},{10,11... | collective-permute-start | bytes 3538952 | tf_op jit(solution)/shard_map/ppermute | solution.py:949
  258.0 36.9 %all-to-all-start.2 = ((bf16[16,72,512]{2,1,0:T(8,128)(2,1)}), bf16[16,72,512]{2,1,0:T(8,128)(2,1)S(1)}, u32[]{:S(2)}, u32[]{:S(2)}) async-start(bf16[16,72,512]{2,1,0:T(8,128)(2,1)} %add_convert_fusion), calls=%async_computation.2 | async-start | bytes 2359296 | tf_op jit(solution)/shard_map/all_to_all | solution.py:945
  264.0 39.9 %collective-permute-start.24 = (bf16[2,512,512]{2,1,0:T(8,128)(2,1)}, bf16[2,512,512]{2,1,0:T(8,128)(2,1)S(1)}, u32[]{:S(2)}, u32[]{:S(2)}) collective-permute-start(bf16[2,512,512]{2,1,0:T(8,128)(2,1)} %join_quarters.1.refs_0_), channel_id=1, source_target_pairs={{0,8},{8,0},{16,24},{24,16},{1,9},{9,1},{17,25},{25,17},{2,10},{10... | collective-permute-start | bytes 3145736 | tf_op jit(solution)/shard_map/ppermute | solution.py:1103
  266.0 38.0 %collective-permute-start.25 = (bf16[2,512,512]{2,1,0:T(8,128)(2,1)}, bf16[2,512,512]{2,1,0:T(8,128)(2,1)S(1)}, u32[]{:S(2)}, u32[]{:S(2)}) collective-permute-start(bf16[2,512,512]{2,1,0:T(8,128)(2,1)} %join_quarters.1.refs_0_), channel_id=1, source_target_pairs={{0,16},{8,24},{16,0},{24,8},{1,17},{9,25},{17,1},{25,9},{2,18},{10... | collective-permute-start | bytes 3145736 | tf_op jit(solution)/shard_map/ppermute | solution.py:1103
  267.4 69.7 %collective-permute-start.26 = (bf16[2,512,512]{2,1,0:T(8,128)(2,1)}, bf16[2,512,512]{2,1,0:T(8,128)(2,1)}, u32[]{:S(2)}, u32[]{:S(2)}) collective-permute-start(bf16[2,512,512]{2,1,0:T(8,128)(2,1)} %join_quarters.1.refs_0_), channel_id=1, source_target_pairs={{0,24},{8,16},{16,8},{24,0},{1,25},{9,17},{17,9},{25,1},{2,26},{10... | collective-permute-start | bytes 3145736 | tf_op jit(solution)/shard_map/ppermute | solution.py:1103
  296.2 46.8 %all-to-all-start.3 = ((bf16[16,72,512]{2,1,0:T(8,128)(2,1)}), bf16[16,72,512]{2,1,0:T(8,128)(2,1)S(1)}, u32[]{:S(2)}, u32[]{:S(2)}) async-start(bf16[16,72,512]{2,1,0:T(8,128)(2,1)} %broadcast_in_dim.2), calls=%async_computation.3 | async-start | bytes 2359296 | tf_op jit(solution)/shard_map/all_to_all | solution.py:945
  343.0 2.9 collective-permute-start.27
  (22 other events, 210.9 us)
where the time goes:
time: 357 us; the launch traced here: 352 us
  Pallas kernels  215 us (60%)
  starting transfers between devices  69.5 us (19%)
  waiting for transfers between devices  50.9 us (14%)
  other arithmetic  7.93 us (2%)
  local copies, waits for them, and re-layouts  5.73 us (2%)
    pallas_call x1, Pallas kernels, attention_backward(): pl.pallas_call(partial(backward_kernel, experts, capacity_rows), out_shap...  67.4 us
    pallas_call x2, Pallas kernels, expert_apply(): pl.pallas_call(partial(expert_kernel, experts, count, len(first)), out_sh...  39.6 us
    ppermute x3, waiting for transfers between devices, share_grads(): lax.ppermute(mine, ('y', 'x'), [(i, i ^ step) for i in range(4)])  37.2 us
    ppermute x14, starting transfers between devices, scatter(): lax.ppermute(piece, ('y', 'x', 'zl'), [(i, i ^ k) for i in range(8)])  26.2 us
    pallas_call x1, Pallas kernels, attention_forward(): pl.pallas_call(partial(forward_kernel, experts), out_shape=(jax.ShapeDtyp...  24.5 us
    ppermute x8, starting transfers between devices, send(): return lax.ppermute(values, self.everyone, pairs)  21 us
    all_to_all x4, starting transfers between devices, spread_out(): return lax.all_to_all(values, axes, split_axis=0, concat_axis=0, tiled=True)  18.6 us
    pallas_call x1, Pallas kernels, expert_grads(): pl.pallas_call(expert_grads_kernel, out_shape=(jax.ShapeDtypeStruct((wide...  15.9 us
  transfers between devices with their start and end apart: 32, of which 6 were waited for; matrix products, arithmetic and copies ran while one was open for 2% of the time, Pallas kernels for 60%

commit v1 on v0

--- a/solution.py
+++ b/solution.py
@@ -124,8 +124,17 @@
     def _():
         low_ref[...] = grad_ref[...].astype(BF16)
 
-    chosen = selector_rows((step ^ mine_ref[0]) * stride, out_ref.shape[1], flat_ref)
-    out_ref[0] = nn(chosen, low_ref[...]).astype(BF16)
+    count, rows, _ = out_ref.shape
+
+    def ahead(n):
+        return selector_rows(((step * count + n) ^ mine_ref[0]) * stride, rows, flat_ref)
+
+    later = ahead(0)
+    for n in range(count):
+        chosen = later
+        if n + 1 < count:
+            later = ahead(n + 1)
+        out_ref[n] = nn(chosen, low_ref[...]).astype(BF16)
 
 
 def dispatch_grad(mine, flat, grad, experts, rows, stride):
@@ -134,8 +143,8 @@
         partial(dispatch_grad_kernel, stride),
         out_shape=jax.ShapeDtypeStruct((experts, rows, D), BF16),
         in_specs=[pl.BlockSpec(memory_space=pltpu.SMEM), whole((8, toks)), whole((toks, D))],
-        out_specs=pl.BlockSpec((1, rows, D), lambda e: (e, 0, 0)),
-        grid=(experts,),
+        out_specs=pl.BlockSpec((4, rows, D), lambda e: (e, 0, 0)),
+        grid=(experts // 4,),
         scratch_shapes=[pltpu.VMEM((toks, D), BF16)],
         compiler_params=params(),
         name="dispatch_grad",
@@ -146,8 +155,12 @@
 
 
 def dispatch_kernel(stride, steps, flat_ref, low_ref, *out_refs):
-    for k, out_ref in zip(steps, out_refs):
-        chosen = selector_rows(k * stride, out_ref.shape[0], flat_ref)
+    rows = out_refs[0].shape[0]
+    later = selector_rows(steps[0] * stride, rows, flat_ref)
+    for n, out_ref in enumerate(out_refs):
+        chosen = later
+        if n + 1 < len(steps):
+            later = selector_rows(steps[n + 1] * stride, rows, flat_ref)
         out_ref[...] = nn(chosen, low_ref[...]).astype(BF16)
 
 
@@ -211,26 +224,33 @@
     hat, _ = standardise(x)
     low_one = (hat * gain_one_ref[...]).astype(BF16)
     packed_ref[...] = nn(low_one, qkv_ref[...]).astype(BF16)
-    for image in range(images):
+    units = [(image, quad) for image in range(images) for quad in range(2)]
+
+    def ahead(image, quad):
         rows = slice(image * PATCHES, (image + 1) * PATCHES)
-        for quad in range(2):
-            cols = slice(quad * QUAD, (quad + 1) * QUAD)
-            queries = packed_ref[rows, quad * QUAD : quad * QUAD + QUAD] * HEAD_DIM ** (-0.5)
-            keys = packed_ref[rows, D + quad * QUAD : D + quad * QUAD + QUAD]
-            values = packed_ref[rows, 2 * D + quad * QUAD : 2 * D + quad * QUAD + QUAD]
-            values_t = jnp.transpose(values)
-            scores = nt(head_stack(keys), queries.astype(BF16))
-            parts = []
-            for h in range(4):
-                own = scores[h * PATCHES : (h + 1) * PATCHES]
-                top = jnp.max(own, axis=0, keepdims=True)
-                weights = jnp.exp(own - top)
-                total = jnp.sum(weights, axis=0, keepdims=True)
-                log_ref[image, quad * 4 + h : quad * 4 + h + 1, :] = top + jnp.log(total)
-                part = nn(values_t[h * HEAD_DIM : (h + 1) * HEAD_DIM], weights.astype(BF16))
-                parts.append(part / total)
-            mixed_t = jnp.concatenate(parts, axis=0)
-            mixed_ref[rows, cols] = jnp.transpose(mixed_t).astype(BF16)
+        at = quad * QUAD
+        queries = (packed_ref[rows, at : at + QUAD] * HEAD_DIM ** (-0.5)).astype(BF16)
+        keys = packed_ref[rows, D + at : D + at + QUAD]
+        values = packed_ref[rows, 2 * D + at : 2 * D + at + QUAD]
+        return jnp.transpose(values), nt(head_stack(keys), queries)
+
+    later = ahead(*units[0])
+    for n, (image, quad) in enumerate(units):
+        values_t, scores = later
+        if n + 1 < len(units):
+            later = ahead(*units[n + 1])
+        parts = []
+        for h in range(4):
+            own = scores[h * PATCHES : (h + 1) * PATCHES]
+            top = jnp.max(own, axis=0, keepdims=True)
+            weights = jnp.exp(own - top)
+            total = jnp.sum(weights, axis=0, keepdims=True)
+            log_ref[image, quad * 4 + h : quad * 4 + h + 1, :] = top + jnp.log(total)
+            part = nn(values_t[h * HEAD_DIM : (h + 1) * HEAD_DIM], weights.astype(BF16))
+            parts.append(part / total)
+        mixed_t = jnp.concatenate(parts, axis=0)
+        rows = slice(image * PATCHES, (image + 1) * PATCHES)
+        mixed_ref[rows, quad * QUAD : (quad + 1) * QUAD] = jnp.transpose(mixed_t).astype(BF16)
     resid = x + nn(mixed_ref[...], out_w_ref[...])
     resid_ref[...] = resid
     hat_two, _ = standardise(resid)
@@ -633,37 +653,44 @@
     out_grad_ref[...] += tn(mixed_ref[...], d_attn)
     d_mixed = nt(d_attn, out_w_ref[...]).astype(BF16)
     scale = HEAD_DIM ** (-0.5)
-    images = log_ref.shape[0]
-    for image in range(images):
+    units = [(image, quad) for image in range(log_ref.shape[0]) for quad in range(2)]
+    lane = lax.broadcasted_iota(jnp.int32, (PATCHES, QUAD), 1) // HEAD_DIM
+
+    def ahead(image, quad):
         rows = slice(image * PATCHES, (image + 1) * PATCHES)
-        for quad in range(2):
-            at = quad * QUAD
-            queries = packed_ref[rows, at : at + QUAD] * scale
-            queries = queries.astype(BF16)
-            keys = packed_ref[rows, D + at : D + at + QUAD]
-            values = packed_ref[rows, 2 * D + at : 2 * D + at + QUAD]
-            grads = d_mixed[rows, at : at + QUAD]
-            scores = nt(head_stack(keys), queries)
-            d_probs = nt(head_stack(values), grads)
-            keys_t = jnp.transpose(keys)
-            lane = lax.broadcasted_iota(jnp.int32, (PATCHES, QUAD), 1) // HEAD_DIM
-            d_values = jnp.zeros((PATCHES, QUAD), F32)
-            d_keys = jnp.zeros((PATCHES, QUAD), F32)
-            parts = []
-            for h in range(4):
-                own = slice(h * PATCHES, (h + 1) * PATCHES)
-                log_row = log_ref[image, quad * 4 + h : quad * 4 + h + 1, :]
-                probs = jnp.exp(scores[own] - log_row)
-                d_own = d_probs[own]
-                inner = jnp.sum(probs * d_own, axis=0, keepdims=True)
-                d_scores = (probs * (d_own - inner)).astype(BF16)
-                d_values = jnp.where(lane == h, nn(probs.astype(BF16), grads), d_values)
-                d_keys = jnp.where(lane == h, nn(d_scores, queries), d_keys)
-                parts.append(nn(keys_t[h * HEAD_DIM : (h + 1) * HEAD_DIM], d_scores))
-            d_queries = jnp.transpose(jnp.concatenate(parts, axis=0)) * scale
-            d_packed_ref[rows, at : at + QUAD] = d_queries.astype(BF16)
-            d_packed_ref[rows, D + at : D + at + QUAD] = d_keys.astype(BF16)
-            d_packed_ref[rows, 2 * D + at : 2 * D + at + QUAD] = d_values.astype(BF16)
+        at = quad * QUAD
+        queries = (packed_ref[rows, at : at + QUAD] * scale).astype(BF16)
+        keys = packed_ref[rows, D + at : D + at + QUAD]
+        values = packed_ref[rows, 2 * D + at : 2 * D + at + QUAD]
+        grads = d_mixed[rows, at : at + QUAD]
+        scores = nt(head_stack(keys), queries)
+        d_probs = nt(head_stack(values), grads)
+        return queries, jnp.transpose(keys), grads, scores, d_probs
+
+    later = ahead(*units[0])
+    for n, (image, quad) in enumerate(units):
+        queries, keys_t, grads, scores, d_probs = later
+        if n + 1 < len(units):
+            later = ahead(*units[n + 1])
+        rows = slice(image * PATCHES, (image + 1) * PATCHES)
+        at = quad * QUAD
+        d_values = jnp.zeros((PATCHES, QUAD), F32)
+        d_keys = jnp.zeros((PATCHES, QUAD), F32)
+        parts = []
+        for h in range(4):
+            own = slice(h * PATCHES, (h + 1) * PATCHES)
+            log_row = log_ref[image, quad * 4 + h : quad * 4 + h + 1, :]
+            probs = jnp.exp(scores[own] - log_row)
+            d_own = d_probs[own]
+            inner = jnp.sum(probs * d_own, axis=0, keepdims=True)
+            d_scores = (probs * (d_own - inner)).astype(BF16)
+            d_values = jnp.where(lane == h, nn(probs.astype(BF16), grads), d_values)
+            d_keys = jnp.where(lane == h, nn(d_scores, queries), d_keys)
+            parts.append(nn(keys_t[h * HEAD_DIM : (h + 1) * HEAD_DIM], d_scores))
+        d_queries = jnp.transpose(jnp.concatenate(parts, axis=0)) * scale
+        d_packed_ref[rows, at : at + QUAD] = d_queries.astype(BF16)
+        d_packed_ref[rows, D + at : D + at + QUAD] = d_keys.astype(BF16)
+        d_packed_ref[rows, 2 * D + at : 2 * D + at + QUAD] = d_values.astype(BF16)
     hat_one, _ = standardise(x_ref[...].astype(F32))
     low_one = (hat_one * gain_one_ref[...]).astype(BF16)
     qkv_grad_ref[...] += tn(low_one, d_packed_ref[...])

time: 357 us -> 351 us (0.983)
  Pallas kernels: 215 us -> 203 us
  starting transfers between devices: 69.5 us -> 76.8 us
    pallas_call x1, Pallas kernels: 67.4 us -> 59.1 us  [attention_backward(): pl.pallas_call(partial(backward_kernel, experts, capacity_rows), out_shap...]
    ppermute x14, starting transfers between devices: 26.2 us -> 31.5 us  [scatter(): lax.ppermute(piece, ('y', 'x', 'zl'), [(i, i ^ k) for i in range(8)])]
    pallas_call x1, Pallas kernels: 24.5 us -> 20.6 us  [attention_forward(): pl.pallas_call(partial(forward_kernel, experts), out_shape=(jax.ShapeDtyp...]
  transfers between devices with their start and end apart: 32 -> 32, of which waited for: 6 -> 6; matrix products, arithmetic and copies ran while one was open for 2% -> 2% of each run, Pallas kernels for 60% -> 57%
where the time goes in v1:
time: 351 us; the launch traced here: 345 us
  Pallas kernels  203 us (58%)
  starting transfers between devices  76.8 us (22%)
  waiting for transfers between devices  50.3 us (14%)
  other arithmetic  7.93 us (2%)
  local copies, waits for them, and re-layouts  5.73 us (2%)
    pallas_call x1, Pallas kernels, attention_backward(): pl.pallas_call(partial(backward_kernel, experts, capacity_rows), out_shap...  59.1 us
    pallas_call x2, Pallas kernels, expert_apply(): pl.pallas_call(partial(expert_kernel, experts, count, len(first)), out_sh...  39.8 us
    ppermute x3, waiting for transfers between devices, share_grads(): lax.ppermute(mine, ('y', 'x'), [(i, i ^ step) for i in range(4)])  37.2 us
    ppermute x14, starting transfers between devices, scatter(): lax.ppermute(piece, ('y', 'x', 'zl'), [(i, i ^ k) for i in range(8)])  31.5 us
    all_to_all x4, starting transfers between devices, spread_out(): return lax.all_to_all(values, axes, split_axis=0, concat_axis=0, tiled=True)  20.8 us
    ppermute x8, starting transfers between devices, send(): return lax.ppermute(values, self.everyone, pairs)  20.8 us
    pallas_call x1, Pallas kernels, attention_forward(): pl.pallas_call(partial(forward_kernel, experts), out_shape=(jax.ShapeDtyp...  20.6 us
    pallas_call x1, Pallas kernels, expert_grads(): pl.pallas_call(expert_grads_kernel, out_shape=(jax.ShapeDtypeStruct((wide...  15.9 us
  transfers between devices with their start and end apart: 32, of which 6 were waited for; matrix products, arithmetic and copies ran while one was open for 2% of the time, Pallas kernels for 57%

profile of v1, /device:TPU:0, one launch (start us, length us, event | category | flops | bytes accessed | tf_op | source)
XLA Modules:
  0.0 345.3 jit_solution(13688216835782891718)
XLA Ops:
  0.7 3.7 %collective-permute-start.4 = (bf16[1,512,2048]{2,1,0:T(8,128)(2,1)}, bf16[1,512,2048]{2,1,0:T(8,128)(2,1)}, u32[]{:S(2)}, u32[]{:S(2)}) collective-permute-start(bf16[1,512,2048]{2,1,0:T(8,128)(2,1)} %refs_6_.3), channel_id=1, source_target_pairs={{0,1},{2,6},{4,5},{6,2},{9,8},{11,14},{13,12},{15,10},{16,20},{18,... | collective-permute-start | bytes 6291464 | tf_op jit(solution)/shard_map/ppermute | solution.py:1077
  8.3 4.1 %route.1 = (s32[8,2304]{1,0:T(8,128)}, s32[2304,8]{1,0:T(8,128)}) custom-call(s32[2,2304]{1,0:T(2,128)} %fusion.2.ids_ref, s32[1,2304]{1,0:T(1,128)} %ranks_ref.1), custom_call_target="tpu_custom_call" | custom-call | flops 1358954496 | bytes 110592 | tf_op jit(solution)/shard_map/route/pallas_call | solution.py:96
  12.4 9.5 %dispatch_grad.1 = bf16[8,288,512]{2,1,0:T(8,128)(2,1)} custom-call(s32[1]{0:T(128)} %bitcast.8.mine_ref, s32[8,2304]{1,0:T(8,128)} %get-tuple-element.112.flat_ref, f32[2304,512]{1,0:T(8,128)} %refs_9_.5), custom_call_target="tpu_custom_call" | custom-call | flops 10871635968 | bytes 7077888 | tf_op jit(solution)/shard_map/dispatch_grad/pallas_call | solution.py:142
  21.9 5.4 %all-to-all-start = ((bf16[8,288,512]{2,1,0:T(8,128)(2,1)}), bf16[8,288,512]{2,1,0:T(8,128)(2,1)S(1)}, u32[]{:S(2)}, u32[]{:S(2)}) async-start(bf16[8,288,512]{2,1,0:T(8,128)(2,1)} %dispatch_grad.1), calls=%async_computation | async-start | bytes 4718592 | tf_op jit(solution)/shard_map/all_to_all | solution.py:972
  28.3 20.6 %attention_forward.1 = (bf16[2304,1536]{1,0:T(8,128)(2,1)}, f32[16,8,144]{2,1,0:T(8,128)}, bf16[2304,512]{1,0:T(8,128)(2,1)}, f32[2304,512]{1,0:T(8,128)}, bf16[...) custom-call(bf16[2304,512]{1,0:T(8,128)(2,1)} %x_ref.3, f32[1,512]{1,0:T(1,128)} %bitcast.37, bf16[512,1536]{1,0:T(8,128)(2,1)} %qkv_w_ref.1, ...), custom_call_target="tpu_custom_call" | custom-call | flops 31000000512 | bytes 23592960 | tf_op jit(solution)/shard_map/attention_forward/pallas_call | solution.py:270
  48.9 5.4 %dispatch.2 = (bf16[288,512]{1,0:T(8,128)(2,1)}, bf16[288,512]{1,0:T(8,128)(2,1)}, bf16[288,512]{1,0:T(8,128)(2,1)}, bf16[288,512]{1,0:T(8,128)(2,1)}) custom-call(s32[8,2304]{1,0:T(8,128)} %get-tuple-element.112.flat_ref, bf16[2304,512]{1,0:T(8,128)(2,1)} %get-tuple-element.107.low_ref.refs_12_), custom_call_target="tpu_custom_call" | custom-call | flops 5435817984 | bytes 4718592 | tf_op jit(solution)/shard_map/dispatch/pallas_call | solution.py:169
  58.2 12.8 %collective-permute-start.10 = (bf16[288,512]{1,0:T(8,128)(2,1)}, bf16[288,512]{1,0:T(8,128)(2,1)S(1)}, u32[]{:S(2)}, u32[]{:S(2)}) collective-permute-start(bf16[288,512]{1,0:T(8,128)(2,1)} %get-tuple-element.127), channel_id=1, source_target_pairs={{0,16},{2,18},{8,24},{10,26},{16,0},{18,2},{24,8},{26,10},{1,17},{... | collective-permute-start | bytes 884744 | tf_op jit(solution)/shard_map/ppermute | solution.py:1067
  73.3 5.4 %dispatch.3 = (bf16[288,512]{1,0:T(8,128)(2,1)}, bf16[288,512]{1,0:T(8,128)(2,1)}, bf16[288,512]{1,0:T(8,128)(2,1)}, bf16[288,512]{1,0:T(8,128)(2,1)}) custom-call(s32[8,2304]{1,0:T(8,128)} %get-tuple-element.112.flat_ref, bf16[2304,512]{1,0:T(8,128)(2,1)} %get-tuple-element.107.low_ref.refs_12_), custom_call_target="tpu_custom_call" | custom-call | flops 5435817984 | bytes 4718592 | tf_op jit(solution)/shard_map/dispatch/pallas_call | solution.py:169
  80.5 3.7 %collective-permute-done.10.refs_3_ = bf16[288,512]{1,0:T(8,128)(2,1)S(1)} collective-permute-done((bf16[288,512]{1,0:T(8,128)(2,1)}, bf16[288,512]{1,0:T(8,128)(2,1)S(1)}, u32[]{:S(2)}, u32[]{:S(2)}) %collective-permute-start.10) | collective-permute-done | bytes 294944 | tf_op jit(solution)/shard_map/ppermute | solution.py:1067
  85.0 3.8 %collective-permute-start.1 = (bf16[288,512]{1,0:T(8,128)(2,1)}, bf16[288,512]{1,0:T(8,128)(2,1)}, u32[]{:S(2)}, u32[]{:S(2)}) collective-permute-start(bf16[288,512]{1,0:T(8,128)(2,1)} %get-tuple-element.118), channel_id=1, source_target_pairs={{0,18},{2,16},{8,26},{10,24},{16,2},{18,0},{24,10},{26,8},{1,19},{... | collective-permute-start | bytes 884744 | tf_op jit(solution)/shard_map/ppermute | solution.py:1067
  92.2 20.0 %expert_apply.2 = (bf16[304,512]{1,0:T(8,128)(2,1)}, bf16[304,512]{1,0:T(8,128)(2,1)}, bf16[304,512]{1,0:T(8,128)(2,1)}, bf16[304,512]{1,0:T(8,128)(2,1)}, bf16[...) custom-call(s32[4]{0:T(128)} %broadcast_xor_fusion.sources_ref, ...), custom_call_target="tpu_custom_call" | custom-call | flops 18119393280 | bytes 9437184 | tf_op jit(solution)/shard_map/expert_apply/pallas_call | solution.py:412
  116.0 19.8 %expert_apply.3 = (bf16[304,512]{1,0:T(8,128)(2,1)}, bf16[304,512]{1,0:T(8,128)(2,1)}, bf16[304,512]{1,0:T(8,128)(2,1)}, bf16[304,512]{1,0:T(8,128)(2,1)}, bf16[...) custom-call(s32[4]{0:T(128)} %broadcast_xor_fusion.1.sources_ref, ...), custom_call_target="tpu_custom_call", output_to_operand_aliasing={{4}: (15, {}), {5}: (16, {}), {6}: (17, {}), {7}: (18, {}),... | custom-call | flops 18119393280 | bytes 9437184 | tf_op jit(solution)/shard_map/expert_apply/pallas_call | solution.py:412
  137.3 2.9 collective-permute-start.15
  142.6 15.9 %expert_grads.1 = (bf16[4,512,512]{2,1,0:T(8,128)(2,1)}, bf16[4,512,512]{2,1,0:T(8,128)(2,1)}) custom-call(s32[1]{0:T(128)} %bitcast.9.core_ref.refs_22_, bf16[2304,512]{1,0:T(8,128)(2,1)} %get-tuple-element.146.low_ref, bf16[2304,512]{1,0:T(8,128)(2,1)} %get-tuple-element.147.d_out_ref, bf16[2304,2048]{1,0:T(8,128)(2,1)} %get-tuple-element.148.hidden_ref, ...), custom_call_target="tpu_custom_call" | custom-call | flops 19327352832 | bytes 18874368 | tf_op jit(solution)/shard_map/expert_grads/pallas_call | solution.py:460
  159.2 2.7 collective-permute-done.16.refs_6_
  163.3 3.6 %all-to-all-start.1 = ((bf16[8,288,512]{2,1,0:T(8,128)(2,1)}), bf16[8,288,512]{2,1,0:T(8,128)(2,1)S(1)}, u32[]{:S(2)}, u32[]{:S(2)}) async-start(bf16[8,288,512]{2,1,0:T(8,128)(2,1)} %get-tuple-element.170), calls=%async_computation.1 | async-start | bytes 4718592 | tf_op jit(solution)/shard_map/all_to_all | solution.py:972
  167.0 5.4 %pair_quarters.1 = (bf16[512,512]{1,0:T(8,128)(2,1)}, bf16[512,512]{1,0:T(8,128)(2,1)}, bf16[512,512]{1,0:T(8,128)(2,1)}, bf16[512,512]{1,0:T(8,128)(2,1)}) custom-call(s32[4]{0:T(128)} %pad_add_fusion.1.picks_ref, bf16[4,512,512]{2,1,0:T(8,128)(2,1)} %get-tuple-element.171.keep_ref, bf16[4,512,512]{2,1,0:T(8,128)(2,1)} %collective-permute-done.18.got_ref), custom_call_target="tpu_custom_call" | custom-call | flops 262144 | bytes 6291456 | tf_op jit(solution)/shard_map/pair_quarters/pallas_call | solution.py:492
  173.0 6.0 %collective-permute-start.20 = (bf16[512,512]{1,0:T(8,128)(2,1)}, bf16[512,512]{1,0:T(8,128)(2,1)}, u32[]{:S(2)}, u32[]{:S(2)}) collective-permute-start(bf16[512,512]{1,0:T(8,128)(2,1)} %get-tuple-element.174), channel_id=1, source_target_pairs={{0,16},{1,24},{2,22},{3,30},{4,20},{5,28},{6,18},{7,26},{8,25},{9,... | collective-permute-start | bytes 1572872 | tf_op jit(solution)/shard_map/ppermute | solution.py:1077
  179.1 2.9 collective-permute-start.21
  182.8 59.1 %attention_backward.1 = (f32[2304,512]{1,0:T(8,128)}, bf16[2304,1536]{1,0:T(8,128)(2,1)}, bf16[16,72,512]{2,1,0:T(8,128)(2,1)}, bf16[16,72,512]{2,1,0:T(8,128)(2,1)}) custom-call(bf16[304,512]{1,0:T(8,128)(2,1)} %get-tuple-element.153.refs_0_, bf16[304,512]{1,0:T(8,128)(2,1)} %copy-done.10, bf16[304,512]{1,0:T(8,128)(2,1)} %copy-done.11, ...), custom_call_target="tpu_custom_call" | custom-call | flops 70000001024 | bytes 23592960 | tf_op jit(solution)/shard_map/attention_backward/pallas_call | solution.py:764
  243.5 3.7 %join_quarters.1.refs_0_ = bf16[2,512,512]{2,1,0:T(8,128)(2,1)} custom-call(s32[3]{0:T(128)} %pad_add_fusion.2.turn_ref, bf16[512,512]{1,0:T(8,128)(2,1)} %copy-done.7, bf16[512,512]{1,0:T(8,128)(2,1)} %collective-permute-done.20.b_ref, bf16[512,512]{1,0:T(8,128)(2,1)} %collective-permute-done.21.c_ref, bf16[512,512]{1,0:T(8,128)(2,1)} %collective-permute-done.22.d_ref, ...), custom_call_target="tpu_custom_call" | custom-call | flops 262144 | bytes 3145728 | tf_op jit(solution)/shard_map/join_quarters/pallas_call | solution.py:528
  247.2 2.6 add_convert_fusion
  249.8 8.0 %all-to-all-start.2 = ((bf16[16,72,512]{2,1,0:T(8,128)(2,1)}), bf16[16,72,512]{2,1,0:T(8,128)(2,1)S(1)}, u32[]{:S(2)}, u32[]{:S(2)}) async-start(bf16[16,72,512]{2,1,0:T(8,128)(2,1)} %add_convert_fusion), calls=%async_computation.2 | async-start | bytes 2359296 | tf_op jit(solution)/shard_map/all_to_all | solution.py:972
  261.4 12.8 %combine.1 = bf16[2304,512]{1,0:T(8,128)(2,1)} custom-call(s32[1]{0:T(128)} %bitcast.8.mine_ref, s32[2304,8]{1,0:T(8,128)} %get-tuple-element.161.refs_8_.flat_ref, bf16[2304,512]{1,0:T(8,128)(2,1)} %bitcast.36, f32[2304,512]{1,0:T(8,128)} %get-tuple-element.162.refs_10_.resid_ref, f32[2304,128]{1,0:T(8,128)} %get-tuple-element.163.refs_11_.router_ref), custom_call_target="tpu_custom_call" | custom-call | flops 1179648 | bytes 1179648 | tf_op jit(solution)/shard_map/combine/pallas_call | solution.py:883
  274.2 10.8 %input_backward.1 = f32[2304,512]{1,0:T(8,128)} custom-call(bf16[2304,1536]{1,0:T(8,128)(2,1)} %get-tuple-element.186.d_packed_ref, f32[2304,512]{1,0:T(8,128)} %get-tuple-element.187.d_resid_ref, bf16[2304,512]{1,0:T(8,128)(2,1)} %x_ref.3, f32[1,512]{1,0:T(1,128)} %bitcast.39, bf16[512,1536]{1,0:T(8,128)(2,1)} %qkv_w_ref.1), custom_call_target="tpu_custom_call" | custom-call | flops 1179648 | bytes 1179648 | tf_op jit(solution)/shard_map/input_backward/pallas_call | solution.py:843
  285.0 3.8 %all-to-all-done.2 = bf16[16,72,512]{2,1,0:T(8,128)(2,1)S(1)} async-done(((bf16[16,72,512]{2,1,0:T(8,128)(2,1)}), bf16[16,72,512]{2,1,0:T(8,128)(2,1)S(1)}, u32[]{:S(2)}, u32[]{:S(2)}) %all-to-all-start.2) | async-done | bytes 1179680 | tf_op jit(solution)/shard_map/all_to_all | solution.py:972
  290.0 3.7 %all-to-all-start.3 = ((bf16[16,72,512]{2,1,0:T(8,128)(2,1)}), bf16[16,72,512]{2,1,0:T(8,128)(2,1)S(1)}, u32[]{:S(2)}, u32[]{:S(2)}) async-start(bf16[16,72,512]{2,1,0:T(8,128)(2,1)} %broadcast_in_dim.2), calls=%async_computation.3 | async-start | bytes 2359296 | tf_op jit(solution)/shard_map/all_to_all | solution.py:972
  293.7 4.0 %collective-permute-done.24.refs_1_ = bf16[2,512,512]{2,1,0:T(8,128)(2,1)S(1)} collective-permute-done((bf16[2,512,512]{2,1,0:T(8,128)(2,1)}, bf16[2,512,512]{2,1,0:T(8,128)(2,1)S(1)}, u32[]{:S(2)}, u32[]{:S(2)}) %collective-permute-start.24) | collective-permute-done | bytes 1048608 | tf_op jit(solution)/shard_map/ppermute | solution.py:1130
  297.7 33.2 %collective-permute-done.26.refs_3_ = bf16[2,512,512]{2,1,0:T(8,128)(2,1)} collective-permute-done((bf16[2,512,512]{2,1,0:T(8,128)(2,1)}, bf16[2,512,512]{2,1,0:T(8,128)(2,1)}, u32[]{:S(2)}, u32[]{:S(2)}) %collective-permute-start.26) | collective-permute-done | bytes 1048608 | tf_op jit(solution)/shard_map/ppermute | solution.py:1130
  330.9 5.8 %unfold.1 = (f32[1,512,2048]{2,1,0:T(8,128)}, f32[1,2048,512]{2,1,0:T(8,128)}) custom-call(s32[1]{0:T(128)} %bitcast.18.corner_ref, bf16[2,512,512]{2,1,0:T(8,128)(2,1)} %join_quarters.1.refs_0_, bf16[2,512,512]{2,1,0:T(8,128)(2,1)} %copy-done.8, bf16[2,512,512]{2,1,0:T(8,128)(2,1)} %copy-done.9, bf16[2,512,512]{2,1,0:T(8,128)(2,1)} %collective-permute-done.26.refs_3_), custom_call_target="tpu_custom_call" | custom-call | flops 104857600000 | bytes 12582912 | tf_op jit(solution)/shard_map/unfold/pallas_call | solution.py:552
  336.8 2.8 collective-permute-done.27.other_ref
  340.7 4.4 %finish.1 = (f32[512,1536]{1,0:T(8,128)}, f32[512,512]{1,0:T(8,128)}, f32[8,512]{1,0:T(8,128)}, f32[1,512]{1,0:T(1,128)}, f32[1,512]{1,0:T(1,128)}) custom-call(s32[1]{0:T(128)} %bitcast.9.core_ref.refs_22_, bf16[16,72,512]{2,1,0:T(8,128)(2,1)} %copy-done.3, bf16[16,72,512]{2,1,0:T(8,128)(2,1)} %copy-done.6, f32[1,512]{1,0:T(1,128)} %bitcast.40, ...), custom_call_target="tpu_custom_call" | custom-call | flops 2097152 | bytes 6291456 | tf_op jit(solution)/shard_map/finish/pallas_call | solution.py:950
  (104 shorter events, 36.0 us)
Async XLA Ops:
  0.7 53.6 %collective-permute-start.4 = (bf16[1,512,2048]{2,1,0:T(8,128)(2,1)}, bf16[1,512,2048]{2,1,0:T(8,128)(2,1)}, u32[]{:S(2)}, u32[]{:S(2)}) collective-permute-start(bf16[1,512,2048]{2,1,0:T(8,128)(2,1)} %refs_6_.3), channel_id=1, source_target_pairs={{0,1},{2,6},{4,5},{6,2},{9,8},{11,14},{13,12},{15,10},{16,20},{18,... | collective-permute-start | bytes 6291464 | tf_op jit(solution)/shard_map/ppermute | solution.py:1077
  4.4 49.8 %collective-permute-start.5 = (bf16[1,2048,512]{2,1,0:T(8,128)(2,1)}, bf16[1,2048,512]{2,1,0:T(8,128)(2,1)}, u32[]{:S(2)}, u32[]{:S(2)}) collective-permute-start(bf16[1,2048,512]{2,1,0:T(8,128)(2,1)} %refs_9_.4), channel_id=1, source_target_pairs={{0,1},{2,7},{4,5},{6,3},{9,8},{11,15},{13,12},{15,11},{16,21},{18,... | collective-permute-start | bytes 6291464 | tf_op jit(solution)/shard_map/ppermute | solution.py:1077
  21.9 68.8 %all-to-all-start = ((bf16[8,288,512]{2,1,0:T(8,128)(2,1)}), bf16[8,288,512]{2,1,0:T(8,128)(2,1)S(1)}, u32[]{:S(2)}, u32[]{:S(2)}) async-start(bf16[8,288,512]{2,1,0:T(8,128)(2,1)} %dispatch_grad.1), calls=%async_computation | async-start | bytes 4718592 | tf_op jit(solution)/shard_map/all_to_all | solution.py:972
  54.2 34.5 %collective-permute-start.6 = (bf16[1,512,2048]{2,1,0:T(8,128)(2,1)}, bf16[1,512,2048]{2,1,0:T(8,128)(2,1)}, u32[]{:S(2)}, u32[]{:S(2)}) collective-permute-start(bf16[1,512,2048]{2,1,0:T(8,128)(2,1)} %collective-permute-done.4.refs_7_), channel_id=1, source_target_pairs={{2,3},{6,7},{10,11},{14,15},{16,17},{20,21},{24,25},{28,29}} | collective-permute-start | bytes 6291464 | tf_op jit(solution)/shard_map/ppermute | solution.py:1077
  56.2 34.6 %collective-permute-start.7 = (bf16[1,2048,512]{2,1,0:T(8,128)(2,1)}, bf16[1,2048,512]{2,1,0:T(8,128)(2,1)}, u32[]{:S(2)}, u32[]{:S(2)}) collective-permute-start(bf16[1,2048,512]{2,1,0:T(8,128)(2,1)} %collective-permute-done.5.refs_10_), channel_id=1, source_target_pairs={{3,2},{7,6},{11,10},{15,14},{17,16},{21,20},{25,24},{29,28}} | collective-permute-start | bytes 6291464 | tf_op jit(solution)/shard_map/ppermute | solution.py:1077
  58.2 25.9 %collective-permute-start.10 = (bf16[288,512]{1,0:T(8,128)(2,1)}, bf16[288,512]{1,0:T(8,128)(2,1)S(1)}, u32[]{:S(2)}, u32[]{:S(2)}) collective-permute-start(bf16[288,512]{1,0:T(8,128)(2,1)} %get-tuple-element.127), channel_id=1, source_target_pairs={{0,16},{2,18},{8,24},{10,26},{16,0},{18,2},{24,8},{26,10},{1,17},{... | collective-permute-start | bytes 884744 | tf_op jit(solution)/shard_map/ppermute | solution.py:1067
  71.0 13.9 %collective-permute-start.8 = (bf16[288,512]{1,0:T(8,128)(2,1)}, bf16[288,512]{1,0:T(8,128)(2,1)S(1)}, u32[]{:S(2)}, u32[]{:S(2)}) collective-permute-start(bf16[288,512]{1,0:T(8,128)(2,1)} %get-tuple-element.125), channel_id=1, source_target_pairs={{0,2},{2,0},{8,10},{10,8},{16,18},{18,16},{24,26},{26,24},{1,3},{3... | collective-permute-start | bytes 884744 | tf_op jit(solution)/shard_map/ppermute | solution.py:1067
  72.4 16.4 %collective-permute-start.9 = (bf16[288,512]{1,0:T(8,128)(2,1)}, bf16[288,512]{1,0:T(8,128)(2,1)}, u32[]{:S(2)}, u32[]{:S(2)}) collective-permute-start(bf16[288,512]{1,0:T(8,128)(2,1)} %get-tuple-element.126), channel_id=1, source_target_pairs={{0,8},{2,10},{8,0},{10,2},{16,24},{18,26},{24,16},{26,18},{1,9},{3... | collective-permute-start | bytes 884744 | tf_op jit(solution)/shard_map/ppermute | solution.py:1067
  84.1 30.5 %collective-permute-start = (bf16[288,512]{1,0:T(8,128)(2,1)}, bf16[288,512]{1,0:T(8,128)(2,1)S(1)}, u32[]{:S(2)}, u32[]{:S(2)}) collective-permute-start(bf16[288,512]{1,0:T(8,128)(2,1)} %get-tuple-element.117), channel_id=1, source_target_pairs={{0,10},{2,8},{8,2},{10,0},{16,26},{18,24},{24,18},{26,16},{1,11},{... | collective-permute-start | bytes 884744 | tf_op jit(solution)/shard_map/ppermute | solution.py:1067
  85.0 30.4 %collective-permute-start.1 = (bf16[288,512]{1,0:T(8,128)(2,1)}, bf16[288,512]{1,0:T(8,128)(2,1)}, u32[]{:S(2)}, u32[]{:S(2)}) collective-permute-start(bf16[288,512]{1,0:T(8,128)(2,1)} %get-tuple-element.118), channel_id=1, source_target_pairs={{0,18},{2,16},{8,26},{10,24},{16,2},{18,0},{24,10},{26,8},{1,19},{... | collective-permute-start | bytes 884744 | tf_op jit(solution)/shard_map/ppermute | solution.py:1067
  88.7 27.2 %collective-permute-start.2 = (bf16[288,512]{1,0:T(8,128)(2,1)}, bf16[288,512]{1,0:T(8,128)(2,1)}, u32[]{:S(2)}, u32[]{:S(2)}) collective-permute-start(bf16[288,512]{1,0:T(8,128)(2,1)} %get-tuple-element.119), channel_id=1, source_target_pairs={{0,24},{2,26},{8,16},{10,18},{16,8},{18,10},{24,0},{26,2},{1,25},{... | collective-permute-start | bytes 884744 | tf_op jit(solution)/shard_map/ppermute | solution.py:1067
  88.8 27.2 %collective-permute-start.3 = (bf16[288,512]{1,0:T(8,128)(2,1)}, bf16[288,512]{1,0:T(8,128)(2,1)}, u32[]{:S(2)}, u32[]{:S(2)}) collective-permute-start(bf16[288,512]{1,0:T(8,128)(2,1)} %get-tuple-element.120), channel_id=1, source_target_pairs={{0,26},{2,24},{8,18},{10,16},{16,10},{18,8},{24,2},{26,0},{1,27},{... | collective-permute-start | bytes 884744 | tf_op jit(solution)/shard_map/ppermute | solution.py:1067
  112.2 28.0 %collective-permute-start.11 = (bf16[304,512]{1,0:T(8,128)(2,1)}, bf16[304,512]{1,0:T(8,128)(2,1)S(1)}, u32[]{:S(2)}, u32[]{:S(2)}) collective-permute-start(bf16[304,512]{1,0:T(8,128)(2,1)} %get-tuple-element.135), channel_id=1, source_target_pairs={{0,2},{2,0},{8,10},{10,8},{16,18},{18,16},{24,26},{26,24},{1,3},{3... | collective-permute-start | bytes 933896 | tf_op jit(solution)/shard_map/ppermute | solution.py:1067
  115.3 24.9 %collective-permute-start.12 = (bf16[304,512]{1,0:T(8,128)(2,1)}, bf16[304,512]{1,0:T(8,128)(2,1)S(1)}, u32[]{:S(2)}, u32[]{:S(2)}) collective-permute-start(bf16[304,512]{1,0:T(8,128)(2,1)} %get-tuple-element.136), channel_id=1, source_target_pairs={{0,8},{2,10},{8,0},{10,2},{16,24},{18,26},{24,16},{26,18},{1,9},{3... | collective-permute-start | bytes 933896 | tf_op jit(solution)/shard_map/ppermute | solution.py:1067
  115.3 27.2 %collective-permute-start.13 = (bf16[304,512]{1,0:T(8,128)(2,1)}, bf16[304,512]{1,0:T(8,128)(2,1)S(1)}, u32[]{:S(2)}, u32[]{:S(2)}) collective-permute-start(bf16[304,512]{1,0:T(8,128)(2,1)} %get-tuple-element.137), channel_id=1, source_target_pairs={{0,16},{2,18},{8,24},{10,26},{16,0},{18,2},{24,8},{26,10},{1,17},{... | collective-permute-start | bytes 933896 | tf_op jit(solution)/shard_map/ppermute | solution.py:1067
  135.8 22.7 %collective-permute-start.14 = (bf16[304,512]{1,0:T(8,128)(2,1)}, bf16[304,512]{1,0:T(8,128)(2,1)S(1)}, u32[]{:S(2)}, u32[]{:S(2)}) collective-permute-start(bf16[304,512]{1,0:T(8,128)(2,1)} %get-tuple-element.141), channel_id=1, source_target_pairs={{0,10},{2,8},{8,2},{10,0},{16,26},{18,24},{24,18},{26,16},{1,11},{... | collective-permute-start | bytes 933896 | tf_op jit(solution)/shard_map/ppermute | solution.py:1067
  137.3 21.9 %collective-permute-start.15 = (bf16[304,512]{1,0:T(8,128)(2,1)}, bf16[304,512]{1,0:T(8,128)(2,1)S(1)}, u32[]{:S(2)}, u32[]{:S(2)}) collective-permute-start(bf16[304,512]{1,0:T(8,128)(2,1)} %get-tuple-element.143), channel_id=1, source_target_pairs={{0,18},{2,16},{8,26},{10,24},{16,2},{18,0},{24,10},{26,8},{1,19},{... | collective-permute-start | bytes 933896 | tf_op jit(solution)/shard_map/ppermute | solution.py:1067
  140.2 21.7 %collective-permute-start.16 = (bf16[304,512]{1,0:T(8,128)(2,1)}, bf16[304,512]{1,0:T(8,128)(2,1)S(1)}, u32[]{:S(2)}, u32[]{:S(2)}) collective-permute-start(bf16[304,512]{1,0:T(8,128)(2,1)} %get-tuple-element.144), channel_id=1, source_target_pairs={{0,24},{2,26},{8,16},{10,18},{16,8},{18,10},{24,0},{26,2},{1,25},{... | collective-permute-start | bytes 933896 | tf_op jit(solution)/shard_map/ppermute | solution.py:1067
  140.3 21.7 %collective-permute-start.17 = (bf16[304,512]{1,0:T(8,128)(2,1)}, bf16[304,512]{1,0:T(8,128)(2,1)S(1)}, u32[]{:S(2)}, u32[]{:S(2)}) collective-permute-start(bf16[304,512]{1,0:T(8,128)(2,1)} %get-tuple-element.145), channel_id=1, source_target_pairs={{0,26},{2,24},{8,18},{10,16},{16,10},{18,8},{24,2},{26,0},{1,27},{... | collective-permute-start | bytes 933896 | tf_op jit(solution)/shard_map/ppermute | solution.py:1067
  161.9 5.0 %collective-permute-start.18 = (bf16[4,512,512]{2,1,0:T(8,128)(2,1)}, bf16[4,512,512]{2,1,0:T(8,128)(2,1)}, u32[]{:S(2)}, u32[]{:S(2)}) collective-permute-start(bf16[4,512,512]{2,1,0:T(8,128)(2,1)} %get-tuple-element.172), channel_id=1, source_target_pairs={{0,1},{1,0},{2,3},{3,2},{4,5},{5,4},{6,7},{7,6},{8,9},{9,8},{10,11... | collective-permute-start | bytes 6291464 | tf_op jit(solution)/shard_map/ppermute | solution.py:1110
  163.3 79.4 %all-to-all-start.1 = ((bf16[8,288,512]{2,1,0:T(8,128)(2,1)}), bf16[8,288,512]{2,1,0:T(8,128)(2,1)S(1)}, u32[]{:S(2)}, u32[]{:S(2)}) async-start(bf16[8,288,512]{2,1,0:T(8,128)(2,1)} %get-tuple-element.170), calls=%async_computation.1 | async-start | bytes 4718592 | tf_op jit(solution)/shard_map/all_to_all | solution.py:972
  172.3 69.6 %collective-permute-start.19 = (bf16[512,512]{1,0:T(8,128)(2,1)}, bf16[512,512]{1,0:T(8,128)(2,1)S(1)}, u32[]{:S(2)}, u32[]{:S(2)}) collective-permute-start(bf16[512,512]{1,0:T(8,128)(2,1)} %get-tuple-element.183.own_a_ref), channel_id=1, source_target_pairs={{1,8},{2,6},{3,14},{5,12},{6,2},{7,10},{8,9},{9,1},{10,15},{11,7},... | collective-permute-start | bytes 1572872 | tf_op jit(solution)/shard_map/ppermute | solution.py:1077
  173.0 68.9 %collective-permute-start.20 = (bf16[512,512]{1,0:T(8,128)(2,1)}, bf16[512,512]{1,0:T(8,128)(2,1)}, u32[]{:S(2)}, u32[]{:S(2)}) collective-permute-start(bf16[512,512]{1,0:T(8,128)(2,1)} %get-tuple-element.174), channel_id=1, source_target_pairs={{0,16},{1,24},{2,22},{3,30},{4,20},{5,28},{6,18},{7,26},{8,25},{9,... | collective-permute-start | bytes 1572872 | tf_op jit(solution)/shard_map/ppermute | solution.py:1077
  179.1 62.8 %collective-permute-start.21 = (bf16[512,512]{1,0:T(8,128)(2,1)}, bf16[512,512]{1,0:T(8,128)(2,1)}, u32[]{:S(2)}, u32[]{:S(2)}) collective-permute-start(bf16[512,512]{1,0:T(8,128)(2,1)} %get-tuple-element.184.own_c_ref), channel_id=1, source_target_pairs={{0,8},{1,0},{2,14},{3,6},{4,12},{5,4},{6,10},{7,2},{8,1},{10,7},{1... | collective-permute-start | bytes 1572872 | tf_op jit(solution)/shard_map/ppermute | solution.py:1077
  181.9 60.7 %collective-permute-start.22 = (bf16[512,512]{1,0:T(8,128)(2,1)}, bf16[512,512]{1,0:T(8,128)(2,1)}, u32[]{:S(2)}, u32[]{:S(2)}) collective-permute-start(bf16[512,512]{1,0:T(8,128)(2,1)} %get-tuple-element.176), channel_id=1, source_target_pairs={{0,24},{1,16},{2,30},{3,22},{4,28},{5,20},{6,26},{7,18},{8,17},{9,... | collective-permute-start | bytes 1572872 | tf_op jit(solution)/shard_map/ppermute | solution.py:1077
  242.7 4.5 %collective-permute-start.23 = (bf16[16,72,512]{2,1,0:T(8,128)(2,1)}, bf16[16,72,512]{2,1,0:T(8,128)(2,1)}, u32[]{:S(2)}, u32[]{:S(2)}) collective-permute-start(bf16[16,72,512]{2,1,0:T(8,128)(2,1)} %get-tuple-element.178), channel_id=1, source_target_pairs={{0,1},{1,0},{2,3},{3,2},{4,5},{5,4},{6,7},{7,6},{8,9},{9,8},{10,11... | collective-permute-start | bytes 3538952 | tf_op jit(solution)/shard_map/ppermute | solution.py:976
  249.8 38.9 %all-to-all-start.2 = ((bf16[16,72,512]{2,1,0:T(8,128)(2,1)}), bf16[16,72,512]{2,1,0:T(8,128)(2,1)S(1)}, u32[]{:S(2)}, u32[]{:S(2)}) async-start(bf16[16,72,512]{2,1,0:T(8,128)(2,1)} %add_convert_fusion), calls=%async_computation.2 | async-start | bytes 2359296 | tf_op jit(solution)/shard_map/all_to_all | solution.py:972
  257.9 39.8 %collective-permute-start.24 = (bf16[2,512,512]{2,1,0:T(8,128)(2,1)}, bf16[2,512,512]{2,1,0:T(8,128)(2,1)S(1)}, u32[]{:S(2)}, u32[]{:S(2)}) collective-permute-start(bf16[2,512,512]{2,1,0:T(8,128)(2,1)} %join_quarters.1.refs_0_), channel_id=1, source_target_pairs={{0,8},{8,0},{16,24},{24,16},{1,9},{9,1},{17,25},{25,17},{2,10},{10... | collective-permute-start | bytes 3145736 | tf_op jit(solution)/shard_map/ppermute | solution.py:1130
  259.8 37.9 %collective-permute-start.25 = (bf16[2,512,512]{2,1,0:T(8,128)(2,1)}, bf16[2,512,512]{2,1,0:T(8,128)(2,1)S(1)}, u32[]{:S(2)}, u32[]{:S(2)}) collective-permute-start(bf16[2,512,512]{2,1,0:T(8,128)(2,1)} %join_quarters.1.refs_0_), channel_id=1, source_target_pairs={{0,16},{8,24},{16,0},{24,8},{1,17},{9,25},{17,1},{25,9},{2,18},{10... | collective-permute-start | bytes 3145736 | tf_op jit(solution)/shard_map/ppermute | solution.py:1130
  261.3 69.7 %collective-permute-start.26 = (bf16[2,512,512]{2,1,0:T(8,128)(2,1)}, bf16[2,512,512]{2,1,0:T(8,128)(2,1)}, u32[]{:S(2)}, u32[]{:S(2)}) collective-permute-start(bf16[2,512,512]{2,1,0:T(8,128)(2,1)} %join_quarters.1.refs_0_), channel_id=1, source_target_pairs={{0,24},{8,16},{16,8},{24,0},{1,25},{9,17},{17,9},{25,1},{2,26},{10... | collective-permute-start | bytes 3145736 | tf_op jit(solution)/shard_map/ppermute | solution.py:1130
  290.0 46.7 %all-to-all-start.3 = ((bf16[16,72,512]{2,1,0:T(8,128)(2,1)}), bf16[16,72,512]{2,1,0:T(8,128)(2,1)S(1)}, u32[]{:S(2)}, u32[]{:S(2)}) async-start(bf16[16,72,512]{2,1,0:T(8,128)(2,1)} %broadcast_in_dim.2), calls=%async_computation.3 | async-start | bytes 2359296 | tf_op jit(solution)/shard_map/all_to_all | solution.py:972
  336.7 2.9 collective-permute-start.27
  (22 other events, 211.2 us)
